TPU v7x, 128 devices: a whole 4x4x4 slice. The times are simulated.
128 devices in a mesh: seq: 16 (over z_lo, x, core), head: 8 (over y, z_hi).
Axes of the slice: x: 4, y: 4, z: 4 (z_hi: 2, z_lo: 2; z = z_hi * 2 + z_lo), core: 2. Of those that a mesh axis runs over, the one named last changes fastest.
Arguments:
- queries: bfloat16 [10240, 5120], P('seq', 'head'), may hold values from -5 to 5
- key_states: bfloat16 [10240, 5120], P('seq', 'head'), may hold values from -5 to 5
- value_states: bfloat16 [10240, 5120], P('seq', 'head'), may hold values from -6 to 6
- tile_mask: int32 [80, 80], replicated, may hold values from 0 to 1, as said below
- out_weight: bfloat16 [5120, 5120], P('head'), may hold values from -0.078125 to 0.078125
- out_bias: float32 [5120], P('head'), may hold values from -1.5 to 1.5
- residual: bfloat16 [10240, 5120], P('seq', 'head'), may hold values from -3 to 3
- gate_scale: float32 [5120], P('head'), may hold values from 0.5 to 2
Outputs:
- block_out: bfloat16 [10240, 5120], P('seq', 'head')
Inputs may be any that keep to these rules, and one draw needn't show every extreme that they name: tile_mask[i, j] is 1 wherever |i - j| <= 3; farther pairs are 1 less often the farther apart they are.
All inputs are finite; a program needn't handle non-finite values.
Results may differ from a plain program's by a relative error of at most 0.009.
Values may be sent and summed in bfloat16 or wider, within the bound.
A program may use at most 128 MiB of HBM per device.

v0:
```python
import jax
import jax.numpy as jnp
from jax import lax
from jax.sharding import PartitionSpec as P

HEAD_DIM = 128
TILE = 128


neg_big = -1e30


def local(queries, key_states, value_states, tile_mask, out_weight, out_bias, residual, gate_scale):
    row_count = queries.shape[0]
    local_heads = queries.shape[1] // HEAD_DIM
    query_tiles = row_count // TILE
    scaling = HEAD_DIM ** (-0.5)
    first_tile = lax.axis_index("seq") * query_tiles
    own_mask = lax.dynamic_slice_in_dim(tile_mask, first_tile, query_tiles, 0) > 0
    row_mask = jnp.repeat(own_mask, TILE, axis=0)
    query_heads = queries.reshape(row_count, local_heads, HEAD_DIM)

    def update(carry, key_piece, value_piece, start):
        maxima, totals, accumulated = carry
        piece_rows = key_piece.shape[0]
        tile_slice = lax.dynamic_slice_in_dim(row_mask, start // TILE, piece_rows // TILE, 1)
        allowed = jnp.repeat(tile_slice, TILE, axis=1)
        key_heads = key_piece.reshape(piece_rows, local_heads, HEAD_DIM)
        value_heads = value_piece.reshape(piece_rows, local_heads, HEAD_DIM)
        scores = (
            jnp.einsum("qhd,khd->hqk", query_heads, key_heads, preferred_element_type=jnp.float32)
            * scaling
        )
        scores = jnp.where(allowed[None], scores, neg_big)
        new_max = jnp.maximum(maxima, jnp.max(scores, axis=2))
        weights = jnp.where(allowed[None], jnp.exp(scores - new_max[:, :, None]), 0.0)
        rescale = jnp.exp(maxima - new_max)
        totals = totals * rescale + jnp.sum(weights, axis=2)
        product = jnp.einsum(
            "hqk,khd->qhd",
            weights.astype(jnp.bfloat16),
            value_heads,
            preferred_element_type=jnp.float32,
        )
        accumulated = accumulated * rescale.T[:, :, None] + product
        return (new_max, totals, accumulated)

    initial = (
        jnp.full((local_heads, row_count), neg_big, jnp.float32),
        jnp.zeros((local_heads, row_count), jnp.float32),
        jnp.zeros((row_count, local_heads, HEAD_DIM), jnp.float32),
    )
    key_piece = lax.all_gather(key_states, "seq", axis=0, tiled=True)
    value_piece = lax.all_gather(value_states, "seq", axis=0, tiled=True)
    piece_rows = key_piece.shape[0]
    block_rows = 512

    def one_block(state_now, block_step):
        block_start = block_step * block_rows
        key_rows = lax.dynamic_slice_in_dim(key_piece, block_start, block_rows, 0)
        value_rows = lax.dynamic_slice_in_dim(value_piece, block_start, block_rows, 0)
        state_next = update(state_now, key_rows, value_rows, block_start)
        return (state_next, None)

    final_state, unused = lax.scan(
        one_block, initial, jnp.arange(piece_rows // block_rows, dtype=jnp.int32)
    )
    maxima, totals, accumulated = final_state
    attended = (
        (accumulated / totals.T[:, :, None])
        .astype(jnp.bfloat16)
        .reshape(row_count, local_heads * HEAD_DIM)
    )
    gathered = lax.all_gather(attended, "head", axis=1, tiled=True)
    weight_rows = lax.all_to_all(out_weight, "head", split_axis=1, concat_axis=0, tiled=True)
    projected = jnp.dot(gathered, weight_rows, preferred_element_type=jnp.float32)
    result = residual.astype(jnp.float32) + gate_scale[None, :] * (projected + out_bias[None, :])
    return result.astype(jnp.bfloat16)


def solution(mesh):
    return jax.shard_map(
        local,
        mesh=mesh,
        in_specs=(
            P("seq", "head"),
            P("seq", "head"),
            P("seq", "head"),
            P(),
            P("head", None),
            P("head"),
            P("seq", "head"),
            P("head"),
        ),
        out_specs=P("seq", "head"),
        check_vma=False,
    )
```

profile of v0, /device:TPU:0, one launch (start us, length us, event | category | flops | bytes accessed | tf_op | source)
XLA Modules:
  0.0 619.4 jit_solution(6216507541371561187)
XLA Ops:
  15.4 70.5 %all-gather.4.cloned.1.call-done = bf16[10240,640]{0,1:T(8,128)(2,1)} async-done(((bf16[640,640]{0,1:T(8,128)(2,1)}), bf16[10240,640]{0,1:T(8,128)(2,1)}) %all-gather.4.cloned.1.call-update) | async-done | bytes 13107216 | tf_op jit(solution)/shard_map/all_gather | solution.py:53
  85.8 76.8 %all-gather.6.cloned.1.call-done = bf16[10240,640]{0,1:T(8,128)(2,1)} async-done(((bf16[640,640]{0,1:T(8,128)(2,1)}), bf16[10240,640]{0,1:T(8,128)(2,1)}) %all-gather.6.cloned.1.call-update) | async-done | bytes 13107216 | tf_op jit(solution)/shard_map/all_gather | solution.py:54
  163.2 292.1 %while.17 = (s32[]{:T(128)}, f32[5,640]{1,0:T(8,128)S(1)}, f32[5,640]{1,0:T(8,128)S(1)}, f32[640,5,128]{0,2,1:T(8,128)S(1)}, s32[20]{0:T(128)}, /*index=5*/pred[...) while((s32[]{:T(128)}, f32[5,640]{1,0:T(8,128)S(1)}, ...), condition=%wide.region_3.4_spmd.clone, body=%wide.region_0.3_spmd.clone.sunk | while | flops 861408000 | bytes 55426996 | solution.py:65
  166.6 4.2 fusion.30
  170.9 5.2 bitcast_add_fusion.2
  181.2 4.2 fusion.30
  185.5 5.2 bitcast_add_fusion.2
  195.8 4.2 fusion.30
  200.1 5.2 bitcast_add_fusion.2
  210.4 4.2 fusion.30
  214.7 5.2 bitcast_add_fusion.2
  225.1 4.2 fusion.30
  229.3 5.2 bitcast_add_fusion.2
  239.7 4.2 fusion.30
  243.9 5.2 bitcast_add_fusion.2
  254.3 4.2 fusion.30
  258.5 5.2 bitcast_add_fusion.2
  268.9 4.2 fusion.30
  273.1 5.2 bitcast_add_fusion.2
  283.5 4.2 fusion.30
  287.7 5.2 bitcast_add_fusion.2
  298.1 4.2 fusion.30
  302.3 5.2 bitcast_add_fusion.2
  312.7 4.2 fusion.30
  316.9 5.2 bitcast_add_fusion.2
  327.3 4.2 fusion.30
  331.5 5.2 bitcast_add_fusion.2
  341.9 4.2 fusion.30
  346.2 5.2 bitcast_add_fusion.2
  356.5 4.2 fusion.30
  360.8 5.2 bitcast_add_fusion.2
  371.1 4.2 fusion.30
  375.4 5.2 bitcast_add_fusion.2
  385.7 4.2 fusion.30
  390.0 5.2 bitcast_add_fusion.2
  400.3 4.2 fusion.30
  404.6 5.2 bitcast_add_fusion.2
  414.9 4.2 fusion.30
  419.2 5.2 bitcast_add_fusion.2
  429.5 4.2 fusion.30
  433.8 5.2 bitcast_add_fusion.2
  444.1 4.2 fusion.30
  448.4 5.2 bitcast_add_fusion.2
  456.3 9.5 %copy.26 = bf16[640,5120]{0,1:T(8,128)(2,1)} copy(bf16[640,5120]{1,0:T(8,128)(2,1)} %param.14) | data formatting | bytes 13107200 | tf_op args[4]
  465.8 102.0 %all_to_all.19 = bf16[640,8,640]{0,2,1:T(8,128)(2,1)} all-to-all(bf16[640,8,640]{0,2,1:T(8,128)(2,1)} %bitcast.67), channel_id=1, replica_groups=mesh['seq'=16,'head'=8] {'head'}, dimensions={1} | all-to-all | bytes 13107200 | tf_op jit(solution)/shard_map/all_to_all | solution.py:75
  567.8 9.5 %copy.27 = bf16[8,640,640]{2,1,0:T(8,128)(2,1)} copy(bf16[8,640,640]{1,2,0:T(8,128)(2,1)} %bitcast.66) | data formatting | bytes 13107200 | tf_op jit(solution)/shard_map/all_to_all | solution.py:75
  577.4 24.6 %all-gather.8.cloned.1.call-done = bf16[640,5120]{0,1:T(8,128)(2,1)} async-done(((bf16[640,640]{0,1:T(8,128)(2,1)}), bf16[640,5120]{0,1:T(8,128)(2,1)}) %all-gather.8.cloned.1.call-update) | async-done | bytes 6553616 | tf_op jit(solution)/shard_map/all_gather | solution.py:74
  601.9 10.9 %add_convert_fusion = bf16[640,640]{1,0:T(8,128)(2,1)} fusion(bf16[640,640]{1,0:T(8,128)(2,1)S(1)} %copy-done.1, bf16[640,5120]{0,1:T(8,128)(2,1)} %all-gather.8.cloned.1.call-done, bf16[5120,640]{1,0:T(8,128)(2,1)} %bitcast.69, f32[640]{0:T(1024)S(1)} %copy-done.2, f32[640]{0:T(1024)S(1)} %copy-done.3), kind=kOutput, calls=%fused_computation.20 | convolution fusion | flops 4196352000 | bytes 14750720 | tf_op jit(solution)/shard_map/dot_general | solution.py:76
  (225 shorter events, 98.0 us)
Async XLA Ops:
  6.5 79.3 %all-gather.4.cloned.1.call-start = ((), (), s32[]{:S(2)}) async-start(), calls=%async_computation.1 | async-start | bytes 13926400 | tf_op jit(solution)/shard_map/all_gather | solution.py:53
  8.7 153.9 %all-gather.6.cloned.1.call-start = ((), (), s32[]{:S(2)}) async-start(), calls=%async_computation.2 | async-start | bytes 13926400 | tf_op jit(solution)/shard_map/all_gather | solution.py:54
  11.0 590.9 %all-gather.8.cloned.1.call-start = ((), (), s32[]{:S(2)}) async-start(), calls=%async_computation.3 | async-start | bytes 7372800 | tf_op jit(solution)/shard_map/all_gather | solution.py:74
  170.9 5.3 copy-start
  185.5 5.3 copy-start
  200.1 5.3 copy-start
  214.7 5.3 copy-start
  229.3 5.3 copy-start
  243.9 5.3 copy-start
  258.5 5.3 copy-start
  273.1 5.3 copy-start
  287.7 5.3 copy-start
  302.3 5.3 copy-start
  316.9 5.3 copy-start
  331.5 5.3 copy-start
  346.1 5.3 copy-start
  360.7 5.3 copy-start
  375.4 5.3 copy-start
  390.0 5.3 copy-start
  404.6 5.3 copy-start
  419.2 5.3 copy-start
  433.8 5.3 copy-start
  448.4 5.3 copy-start
  567.8 34.1 %copy-start.1 = (bf16[640,640]{1,0:T(8,128)(2,1)S(1)}, bf16[640,640]{1,0:T(8,128)(2,1)}, u32[]{:S(2)}) copy-start(bf16[640,640]{1,0:T(8,128)(2,1)} %param.16) | copy-start | bytes 2457604
  567.8 34.1 %copy-start.2 = (f32[640]{0:T(1024)S(1)}, f32[640]{0:T(1024)}, u32[]{:S(2)}) copy-start(f32[640]{0:T(1024)} %param.15) | copy-start | bytes 7684
  567.8 34.1 %copy-start.3 = (f32[640]{0:T(1024)S(1)}, f32[640]{0:T(1024)}, u32[]{:S(2)}) copy-start(f32[640]{0:T(1024)} %param.17) | copy-start | bytes 7684
Sparse Core Ops, SparseCore 0:
  9.0 76.7 all-gather.3
  87.5 75.1 all-gather.5
  456.5 145.4 all-gather.7
where the time goes:
time: 622 us; the launch traced here: 619 us
  matrix products  200 us (32%)
  waiting for transfers between devices  172 us (28%)
  blocking collectives  102 us (16%)
  local copies, waits for them, and re-layouts  82.6 us (13%)
  other arithmetic  34.2 us (5%)
  loops' own time  15 us (2%)
  between operations  13.2 us (2%)
    dot_general x20, matrix products, update(): jnp.einsum('hqk,khd->qhd', weights.astype(jnp.bfloat16), value_heads, pre...  105 us
    all_to_all x1, blocking collectives, local(): lax.all_to_all(out_weight, 'head', split_axis=1, concat_axis=0, tiled=True)  102 us
    dot_general x20, matrix products, update(): jnp.einsum('qhd,khd->hqk', query_heads, key_heads, preferred_element_type...  84.5 us
    all_gather x1, waiting for transfers between devices, local(): value_piece = lax.all_gather(value_states, 'seq', axis=0, tiled=True)  76.8 us
    all_gather x1, waiting for transfers between devices, local(): key_piece = lax.all_gather(key_states, 'seq', axis=0, tiled=True)  70.5 us
    reduce_sum x20, other arithmetic, update(): totals = totals * rescale + jnp.sum(weights, axis=2)  31.9 us
    dynamic_slice x20, local copies, waits for them, and re-layouts, one_block(): lax.dynamic_slice_in_dim(value_piece, block_start, block_rows, 0)  27.6 us
    dynamic_slice x20, local copies, waits for them, and re-layouts, local(): lax.scan(one_block, initial, jnp.arange(piece_rows // block_rows, dtype=j...  25.2 us
  transfers between devices with their start and end apart: 3, of which 3 were waited for; matrix products, arithmetic and copies ran while one was open for 4% of the time, Pallas kernels for 0%

commit v1 on v0

v1 whole, which is shorter than its diff:
```python
import jax
import jax.numpy as jnp
from jax import lax
from jax.experimental import pallas as pl
from jax.experimental.pallas import tpu as pltpu
from jax.sharding import PartitionSpec as P

HEAD_DIM = 128
TILE = 128
ROWS = 640
ROW_TILES = ROWS // TILE
SEQ = 16
RING = 4
TILE_COUNT = 80
MESH = pl.DeviceIdType.MESH
MASKED = -1e30


def place():
    s = lax.axis_index("seq")
    h = lax.axis_index("head")
    return lax.div(s, 8), lax.rem(lax.div(s, 2), 4), lax.rem(s, 2), lax.div(h, 2), lax.rem(h, 2)


def gather_kernel(
    q_ref, k_ref, v_ref, w_ref, kv_out, q_out, w_out,
    stage, stage_sem, local_sem, send_sem, z_sem, x_sem, far_sem, sib_sem, w_sem, w_sib_sem,
):
    zl, x, core, y, zh = place()
    other = 1 - zl
    right, left = lax.rem(x + 1, RING), lax.rem(x + 3, RING)
    opposite = lax.rem(x + 2, RING)

    def seq_of(zl_, x_, core_):
        return (zl_ * RING + x_) * 2 + core_

    head_me = y * 2 + zh
    me = seq_of(zl, x, core)
    to_pair = (seq_of(other, x, core), head_me)
    to_right = (seq_of(zl, right, core), head_me)
    to_left = (seq_of(zl, left, core), head_me)
    to_sib = (seq_of(zl, x, 1 - core), head_me)
    to_y = [(me, lax.rem(y + d, RING) * 2 + zh) for d in (1, 2, 3)]

    barrier = pltpu.get_barrier_semaphore()
    neighbours = [to_pair, to_right, to_left, to_sib] + to_y
    for n in neighbours:
        pl.semaphore_signal(barrier, inc=1, device_id=n, device_id_type=MESH)

    def head_columns(h):
        return pl.ds(pl.multiple_of(h * HEAD_DIM, HEAD_DIM), HEAD_DIM)

    staged = []
    for plane, base in ((zl, 0), (other, 6)):
        for j in range(2):
            staged.append((k_ref, plane * 2 + j, base + 2 * j))
            staged.append((v_ref, plane * 2 + j, base + 2 * j + 1))
    staged += [(k_ref, 4, 4), (v_ref, 4, 5), (q_ref, other * 2, 10), (q_ref, other * 2 + 1, 11)]
    stage_copies = [
        pltpu.make_async_copy(src.at[:, head_columns(h)], stage.at[at], stage_sem.at[at]) for src, h, at in staged
    ]
    for c in stage_copies:
        c.start()
    half = pl.ds(pl.multiple_of(core * (ROWS // 2), ROWS // 2), ROWS // 2)
    other_half = pl.ds(pl.multiple_of((1 - core) * (ROWS // 2), ROWS // 2), ROWS // 2)

    def panel(y_):
        return pl.ds(pl.multiple_of(y_ * (2 * ROWS), 2 * ROWS), 2 * ROWS)

    local = [
        pltpu.make_async_copy(q_ref.at[:, head_columns(zl * 2)], q_out.at[0], local_sem.at[0]),
        pltpu.make_async_copy(q_ref.at[:, head_columns(zl * 2 + 1)], q_out.at[1], local_sem.at[1]),
        pltpu.make_async_copy(q_ref.at[:, head_columns(4)], q_out.at[2], local_sem.at[2]),
        pltpu.make_async_copy(w_ref.at[half, panel(y)], w_out.at[y, half], local_sem.at[3]),
    ]
    for c in local:
        c.start()
    for c in stage_copies:
        c.wait()
    own = pltpu.make_async_copy(stage.at[pl.ds(0, 6)], kv_out.at[me], local_sem.at[4])
    own.start()
    pl.semaphore_wait(barrier, len(neighbours))

    sends = []

    def send(src, dst, recv, target):
        c = pltpu.make_async_remote_copy(
            src_ref=src, dst_ref=dst, send_sem=send_sem.at[len(sends)], recv_sem=recv, device_id=target, device_id_type=MESH
        )
        c.start()
        sends.append(c)

    def arrived(dst, recv, source):
        pltpu.make_async_remote_copy(
            src_ref=dst, dst_ref=dst, send_sem=send_sem.at[0], recv_sem=recv, device_id=source, device_id_type=MESH
        ).wait_recv()

    A, B, H = pl.ds(0, 2), pl.ds(2, 2), pl.ds(4, 2)
    H0, H1 = pl.ds(4, 1), pl.ds(5, 1)
    sib_waits = []

    def to_sibling(origin_zl, origin_x, part):
        n = len(sib_waits)
        block = kv_out.at[seq_of(origin_zl, origin_x, core), part]
        send(block, block, sib_sem.at[n], to_sib)
        sib_waits.append((origin_zl, origin_x, part))

    def pass_on(origin_zl, origin_x, part, recv, target):
        block = kv_out.at[seq_of(origin_zl, origin_x, core), part]
        send(block, block, recv, target)

    def block_of(origin_zl, origin_x, part):
        return kv_out.at[seq_of(origin_zl, origin_x, core), part]

    send(stage.at[pl.ds(6, 2)], kv_out.at[me, A], z_sem.at[0], to_pair)
    send(stage.at[pl.ds(8, 2)], kv_out.at[me, B], z_sem.at[1], to_pair)
    for item, part, at in ((0, H, 4), (1, A, 0), (2, B, 2)):
        send(stage.at[pl.ds(at, 2)], kv_out.at[me, part], x_sem.at[0, item], to_right)
        send(stage.at[pl.ds(at, 2)], kv_out.at[me, part], x_sem.at[1, item], to_left)
    for d in range(3):
        send(w_ref.at[half, panel(lax.rem(y + d + 1, RING))], w_out.at[y, half], w_sem.at[d], to_y[d])
    own.wait()
    to_sibling(zl, x, pl.ds(0, 6))

    for item, part, n in ((3, A, 0), (4, B, 1)):
        arrived(block_of(other, x, part), z_sem.at[n], to_pair)
        pass_on(other, x, part, x_sem.at[0, item], to_right)
        pass_on(other, x, part, x_sem.at[1, item], to_left)
        if n == 0:
            send(stage.at[pl.ds(4, 2)], kv_out.at[me, H], z_sem.at[2], to_pair)
        else:
            send(stage.at[pl.ds(10, 2)], q_out.at[pl.ds(3, 2)], z_sem.at[3], to_pair)
        to_sibling(other, x, part)

    def from_left(item, zl_, part):
        arrived(block_of(zl_, left, part), x_sem.at[0, item], to_left)

    def from_right(item, zl_, part):
        arrived(block_of(zl_, right, part), x_sem.at[1, item], to_right)

    from_left(0, zl, H)
    pass_on(zl, left, H0, far_sem.at[0, 0], to_right)
    pass_on(zl, left, H, z_sem.at[4], to_pair)
    to_sibling(zl, left, H)
    from_right(0, zl, H)
    pass_on(zl, right, H1, far_sem.at[1, 0], to_left)
    pass_on(zl, right, H, z_sem.at[5], to_pair)
    to_sibling(zl, right, H)

    for item, zl_, far in ((1, zl, 1), (3, other, 2)):
        from_left(item, zl_, A)
        pass_on(zl_, left, A, far_sem.at[0, far], to_right)
        to_sibling(zl_, left, A)
        from_right(item, zl_, A)
        to_sibling(zl_, right, A)
        from_right(item + 1, zl_, B)
        pass_on(zl_, right, B, far_sem.at[1, far], to_left)
        to_sibling(zl_, right, B)
        from_left(item + 1, zl_, B)
        to_sibling(zl_, left, B)
        if far == 1:
            arrived(block_of(zl, opposite, H0), far_sem.at[0, 0], to_left)
            arrived(block_of(zl, opposite, H1), far_sem.at[1, 0], to_right)
            pass_on(zl, opposite, H, z_sem.at[6], to_pair)
            to_sibling(zl, opposite, H)
            arrived(block_of(other, x, H), z_sem.at[2], to_pair)
            to_sibling(other, x, H)
    for d in range(3):
        y_ = lax.rem(y + 3 - d, RING)
        arrived(w_out.at[y_, half], w_sem.at[d], to_y[2 - d])
    for d in range(4):
        y_ = lax.rem(y + d, RING)
        if d == 0:
            local[3].wait()
        send(w_out.at[y_, half], w_out.at[y_, half], w_sib_sem.at[d], to_sib)
    for zl_, far in ((zl, 1), (other, 2)):
        arrived(block_of(zl_, opposite, A), far_sem.at[0, far], to_left)
        to_sibling(zl_, opposite, A)
        arrived(block_of(zl_, opposite, B), far_sem.at[1, far], to_right)
        to_sibling(zl_, opposite, B)
    for n, x_ in ((4, left), (5, right), (6, opposite)):
        arrived(block_of(other, x_, H), z_sem.at[n], to_pair)
        to_sibling(other, x_, H)
    arrived(q_out.at[pl.ds(3, 2)], z_sem.at[3], to_pair)
    for d in range(4):
        y_ = lax.rem(y + d, RING)
        arrived(w_out.at[y_, other_half], w_sib_sem.at[d], to_sib)
    for n, (zl_, x_, part) in enumerate(sib_waits):
        arrived(kv_out.at[seq_of(zl_, x_, 1 - core), part], sib_sem.at[n], to_sib)
    for c in sends:
        c.wait_send()
    for c in local[:3]:
        c.wait()


def gather(q, k, v, w):
    bf16 = jnp.bfloat16
    return pl.pallas_call(
        gather_kernel,
        out_shape=[
            jax.ShapeDtypeStruct((SEQ, 6, ROWS, HEAD_DIM), bf16),
            jax.ShapeDtypeStruct((5, ROWS, HEAD_DIM), bf16),
            jax.ShapeDtypeStruct((RING, ROWS, 2 * ROWS), bf16),
        ],
        in_specs=[pl.BlockSpec(memory_space=pl.ANY)] * 4,
        out_specs=[pl.BlockSpec(memory_space=pl.ANY)] * 3,
        scratch_shapes=[
            pltpu.VMEM((12, ROWS, HEAD_DIM), bf16),
            pltpu.SemaphoreType.DMA((12,)),
            pltpu.SemaphoreType.DMA((5,)),
            pltpu.SemaphoreType.DMA((64,)),
            pltpu.SemaphoreType.DMA((7,)),
            pltpu.SemaphoreType.DMA((2, 5)),
            pltpu.SemaphoreType.DMA((2, 3)),
            pltpu.SemaphoreType.DMA((24,)),
            pltpu.SemaphoreType.DMA((3,)),
            pltpu.SemaphoreType.DMA((4,)),
        ],
        compiler_params=pltpu.CompilerParams(collective_id=0, has_side_effects=True),
        name="gather_heads",
    )(q, k, v, w)


GROUP = 4


def attend_kernel(tiles_ref, counts_ref, q_ref, k_ref, v_ref, o_ref, scores):
    j = pl.program_id(0)
    scaling = HEAD_DIM ** -0.5

    def one_row(i, _):
        mine = i < ROW_TILES
        slot = jnp.where(mine, j, 3 + j)
        rows = pl.ds(pl.multiple_of(jnp.where(mine, i, i - ROW_TILES) * TILE, TILE), TILE)
        q = q_ref[slot, rows, :]
        count = counts_ref[i]
        groups = lax.div(count + (GROUP - 1), GROUP)

        def tile_of(ref, n):
            t = tiles_ref[i, n]
            owner = lax.div(t, ROW_TILES)
            return ref[owner, 0, pl.ds(pl.multiple_of((t - owner * ROW_TILES) * TILE, TILE), TILE), :]

        def score(g, peak):
            keys = jnp.concatenate([tile_of(k_ref, g * GROUP + t) for t in range(GROUP)], axis=0)
            s = lax.dot_general(q, keys, (((1,), (1,)), ((), ())), preferred_element_type=jnp.float32)
            for t in range(GROUP):
                part = jnp.where(g * GROUP + t < count, s[:, t * TILE : (t + 1) * TILE], MASKED)
                scores[g * GROUP + t] = part
                peak = jnp.maximum(peak, part)
            return peak

        peak = lax.fori_loop(0, groups, score, jnp.full((TILE, TILE), MASKED, jnp.float32))
        row_max = jnp.max(peak, axis=1, keepdims=True)

        def blend(g, carry):
            total, acc = carry
            values = jnp.concatenate([tile_of(v_ref, g * GROUP + t) for t in range(GROUP)], axis=0)
            weights = [jnp.exp((scores[g * GROUP + t] - row_max) * scaling) for t in range(GROUP)]
            for part in weights:
                total = total + part
            w = jnp.concatenate(weights, axis=1).astype(jnp.bfloat16)
            return total, acc + jnp.dot(w, values, preferred_element_type=jnp.float32)

        zero = jnp.zeros((TILE, HEAD_DIM), jnp.float32)
        total, acc = lax.fori_loop(0, groups, blend, (zero, zero))
        o_ref[slot, rows, :] = (acc / jnp.sum(total, axis=1, keepdims=True)).astype(o_ref.dtype)
        return 0

    lax.fori_loop(0, jnp.where(j < 2, 2 * ROW_TILES, ROW_TILES), one_row, 0)


def attend(tiles, counts, q, kv):
    return pl.pallas_call(
        attend_kernel,
        out_shape=jax.ShapeDtypeStruct((5, ROWS, HEAD_DIM), jnp.bfloat16),
        grid_spec=pltpu.PrefetchScalarGridSpec(
            num_scalar_prefetch=2,
            grid=(3,),
            in_specs=[
                pl.BlockSpec((5, ROWS, HEAD_DIM), lambda j, *_: (0, 0, 0)),
                pl.BlockSpec((SEQ, 1, ROWS, HEAD_DIM), lambda j, *_: (0, 2 * j, 0, 0)),
                pl.BlockSpec((SEQ, 1, ROWS, HEAD_DIM), lambda j, *_: (0, 2 * j + 1, 0, 0)),
            ],
            out_specs=pl.BlockSpec((5, ROWS, HEAD_DIM), lambda j, *_: (0, 0, 0)),
            scratch_shapes=[pltpu.VMEM((TILE_COUNT, TILE, TILE), jnp.float32)],
        ),
        compiler_params=pltpu.CompilerParams(vmem_limit_bytes=48 << 20),
        name="attend",
    )(tiles, counts, q, kv, kv)


def tile_lists(tile_mask):
    zl, x, core, _, _ = place()
    own = (zl * RING + x) * 2 + core
    pair = ((1 - zl) * RING + x) * 2 + core
    rows = jnp.concatenate(
        [lax.dynamic_slice_in_dim(tile_mask, first * ROW_TILES, ROW_TILES, 0) for first in (own, pair)], axis=0
    )
    allowed = rows > 0
    at = jnp.arange(TILE_COUNT, dtype=jnp.int32)
    before = jnp.sum(jnp.where(allowed[:, None, :] & (at[None, None, :] < at[None, :, None]), 1, 0), axis=2)
    hit = allowed[:, None, :] & (before[:, None, :] == at[None, :, None])
    tiles = jnp.sum(jnp.where(hit, at[None, None, :], 0), axis=2)
    return tiles.astype(jnp.int32), jnp.sum(allowed, axis=1).astype(jnp.int32)


def local(queries, key_states, value_states, tile_mask, out_weight, out_bias, residual, gate_scale):
    zl, x, core, y, zh = place()
    tiles, counts = tile_lists(tile_mask)
    kv, q, panel = gather(queries, key_states, value_states, out_weight)
    o = attend(tiles, counts, q, kv)
    pairs = [(s, (s + 8) % 16) for s in range(SEQ)]
    back = lax.ppermute(o[3:5], "seq", pairs)
    low = jnp.where(zl == 0, o[0:2], back)
    high = jnp.where(zl == 0, back, o[0:2])
    attended = jnp.concatenate([low, high, o[2:3]], axis=0).transpose(1, 0, 2).reshape(ROWS, ROWS)
    gathered = lax.all_gather(
        attended, "head", axis=1, tiled=True, axis_index_groups=[[0, 2, 4, 6], [1, 3, 5, 7]]
    )
    partial = jnp.dot(gathered, panel.reshape(RING * ROWS, 2 * ROWS), preferred_element_type=jnp.float32)
    mine = lax.dynamic_slice_in_dim(partial, zh * ROWS, ROWS, 1)
    theirs = lax.dynamic_slice_in_dim(partial, (1 - zh) * ROWS, ROWS, 1).astype(jnp.bfloat16)
    projected = mine + lax.ppermute(theirs, "head", [(h, h ^ 1) for h in range(8)]).astype(jnp.float32)
    result = residual.astype(jnp.float32) + gate_scale[None, :] * (projected + out_bias[None, :])
    return result.astype(jnp.bfloat16)


def solution(mesh):
    return jax.shard_map(
        local,
        mesh=mesh,
        in_specs=(
            P("seq", "head"),
            P("seq", "head"),
            P("seq", "head"),
            P(),
            P("head", None),
            P("head"),
            P("seq", "head"),
            P("head"),
        ),
        out_specs=P("seq", "head"),
        check_vma=False,
    )
```

time: 622 us -> 240 us (0.39)
  matrix products: 200 us -> 8.37 us
  Pallas kernels: 0 us -> 128 us
  blocking collectives: 102 us -> 0 us
  waiting for transfers between devices: 172 us -> 73.4 us
  local copies, waits for them, and re-layouts: 82.6 us -> 4.65 us
  other arithmetic: 34.2 us -> 3.42 us
  loops' own time: 15 us -> 0 us
  starting transfers between devices: 0.09 us -> 8.09 us
    dot_general x41 -> x1, matrix products: 200 us -> 8.37 us  [local(): jnp.dot(gathered, panel.reshape(RING * ROWS, 2 * ROWS), preferred_element...]
    pallas_call x0 -> x2, Pallas kernels: none -> 128 us  [the longest x1 64.4 us: attend(): pl.pallas_call(attend_kernel, out_shape=jax.ShapeDtypeStruct((5, ROWS, HE...]
    all_gather x3 -> x1, waiting for transfers between devices: 172 us -> 47.6 us  [local(): lax.all_gather(attended, 'head', axis=1, tiled=True, axis_index_groups=[[...]
    all_to_all x1 -> x0, blocking collectives: 102 us -> none  [local(): lax.all_to_all(out_weight, 'head', split_axis=1, concat_axis=0, tiled=True)]
    dynamic_slice x60 -> x1, local copies, waits for them, and re-layouts: 53.2 us -> 0.73 us  [tile_lists(): lax.dynamic_slice_in_dim(tile_mask, first * ROW_TILES, ROW_TILES, 0)]
    reduce_sum x20 -> x3, other arithmetic: 31.9 us -> 0.62 us  [the longest x1 0.25 us: tile_lists(): jnp.sum(jnp.where(allowed[:, None, :] & (at[None, None, :] < at[None, :,...]
    ppermute x0 -> x2, waiting for transfers between devices: none -> 25.7 us  [the longest x1 18.7 us: local(): lax.ppermute(theirs, 'head', [(h, h ^ 1) for h in range(8)])]
    unnamed x12 -> x6, local copies, waits for them, and re-layouts: 17.1 us -> 1.15 us
  transfers between devices with their start and end apart: 3 -> 3, of which waited for: 3 -> 3; matrix products, arithmetic and copies ran while one was open for 4% -> 0% of each run, Pallas kernels for 0% -> 0%
where the time goes in v1:
time: 240 us
  Pallas kernels  128 us (53%)
  waiting for transfers between devices  73.4 us (31%)
  between operations  13.5 us (6%)
  matrix products  8.37 us (3%)
  starting transfers between devices  8.09 us (3%)
  local copies, waits for them, and re-layouts  4.65 us (2%)
  other arithmetic  3.42 us (1%)
    pallas_call x1, Pallas kernels, attend(): pl.pallas_call(attend_kernel, out_shape=jax.ShapeDtypeStruct((5, ROWS, HE...  64.4 us
    pallas_call x1, Pallas kernels, gather(): pl.pallas_call(gather_kernel, out_shape=[jax.ShapeDtypeStruct((SEQ, 6, RO...  64 us
    all_gather x1, waiting for transfers between devices, local(): lax.all_gather(attended, 'head', axis=1, tiled=True, axis_index_groups=[[...  47.6 us
    ppermute x1, waiting for transfers between devices, local(): lax.ppermute(theirs, 'head', [(h, h ^ 1) for h in range(8)])  18.7 us
    dot_general x1, matrix products, local(): jnp.dot(gathered, panel.reshape(RING * ROWS, 2 * ROWS), preferred_element...  8.37 us
    ppermute x1, waiting for transfers between devices, local(): back = lax.ppermute(o[3:5], 'seq', pairs)  7.06 us
    ppermute x1, starting transfers between devices, local(): back = lax.ppermute(o[3:5], 'seq', pairs)  4.94 us
  transfers between devices with their start and end apart: 3, of which 3 were waited for; matrix products, arithmetic and copies ran while one was open for 0% of the time, Pallas kernels for 0%

profile of v1, /device:TPU:0, one launch (start us, length us, event | category | flops | bytes accessed | tf_op | source)
XLA Modules:
  0.0 239.8 jit_solution(9265520033138091219)
XLA Ops:
  6.5 0.0 all-gather.2.cloned.1.call-start
  6.6 0.7 constant_dynamic-slice_fusion.1
  7.3 0.1 convert_reduce_fusion
  7.4 0.2 select_reduce_fusion.1
  7.7 0.2 select_reduce_fusion.tiles_ref
  7.9 64.0 %gather_heads.1 = (bf16[16,6,640,128]{3,2,1,0:T(8,128)(2,1)}, bf16[5,640,128]{2,1,0:T(8,128)(2,1)}, bf16[4,640,1280]{2,1,0:T(8,128)(2,1)}) custom-call(bf16[640,640]{1,0:T(8,128)(2,1)} %q_ref.1, bf16[640,640]{1,0:T(8,128)(2,1)} %k_ref.1, bf16[640,640]{1,0:T(8,128)(2,1)} %v_ref.1, bf16[640,5120]{1,0:T(8,128)(2,1)} %w_ref.1), custom_call_target="tpu_custom_call" | custom-call | tf_op jit(solution)/shard_map/gather_heads/pallas_call | solution.py:198
  72.0 0.0 copy-start
  72.0 1.1 copy-done
  73.1 64.4 %attend.1 = bf16[5,640,128]{2,1,0:T(8,128)(2,1)S(1)} custom-call(s32[10,80]{1,0:T(8,128)S(1)} %select_reduce_fusion.tiles_ref, s32[10]{0:T(128)S(1)} %get-tuple-element.11.counts_ref, bf16[5,640,128]{2,1,0:T(8,128)(2,1)S(1)} %copy-done, bf16[16,6,640,128]{3,2,1,0:T(8,128)(2,1)} %get-tuple-element.9.k_ref.v_ref, ...), custom_call_target="tpu_custom_call" | custom-call | tf_op jit(solution)/shard_map/attend/pallas_call | solution.py:274
  137.6 4.9 %collective-permute-start = (bf16[2,640,128]{2,1,0:T(8,128)(2,1)S(1)}, bf16[2,640,128]{2,1,0:T(8,128)(2,1)S(1)}, u32[]{:S(2)}, u32[]{:S(2)}) collective-permute-start(bf16[2,640,128]{2,1,0:T(8,128)(2,1)S(1)} %slice.14), channel_id=1, source_target_pairs={{0,64},{8,72},{16,80},{24,88},{32,96},{40,104},{48,112},{56,120},{... | collective-permute-start | bytes 983048 | tf_op jit(solution)/shard_map/ppermute | solution.py:314
  142.5 7.1 %collective-permute-done = bf16[2,640,128]{2,1,0:T(8,128)(2,1)S(1)} collective-permute-done((bf16[2,640,128]{2,1,0:T(8,128)(2,1)S(1)}, bf16[2,640,128]{2,1,0:T(8,128)(2,1)S(1)}, u32[]{:S(2)}, u32[]{:S(2)}) %collective-permute-start) | collective-permute-done | bytes 327712 | tf_op jit(solution)/shard_map/ppermute | solution.py:314
  149.6 0.1 maximum_bitcast_fusion
  149.7 1.8 copy.10
  151.5 0.0 all-gather.2.cloned.1.call-update
  151.5 47.6 %all-gather.2.cloned.1.call-done = bf16[640,2560]{0,1:T(8,128)(2,1)} async-done(((bf16[640,640]{0,1:T(8,128)(2,1)}), bf16[640,2560]{0,1:T(8,128)(2,1)}) %all-gather.2.cloned.1.call-update) | async-done | bytes 3276816 | tf_op jit(solution)/shard_map/all_gather | solution.py:318
  199.1 0.0 copy-start.1
  199.1 0.0 copy-start.2
  199.1 8.4 %fusion.1 = f32[640,1280]{1,0:T(8,128)S(1)} fusion(bf16[640,2560]{0,1:T(8,128)(2,1)} %all-gather.2.cloned.1.call-done, bf16[2560,1280]{1,0:T(8,128)(2,1)} %bitcast.7), kind=kOutput, calls=%fused_computation.14 | convolution fusion | flops 4194304000 | bytes 13107200 | tf_op jit(solution)/shard_map/dot_general | solution.py:321
  207.5 1.0 dynamic-slice_convert_fusion
  208.5 3.1 %collective-permute-start.1 = (bf16[640,640]{1,0:T(8,128)(2,1)}, bf16[640,640]{1,0:T(8,128)(2,1)}, u32[]{:S(2)}, u32[]{:S(2)}) collective-permute-start(bf16[640,640]{1,0:T(8,128)(2,1)} %dynamic-slice_convert_fusion), channel_id=1, source_target_pairs={{0,1},{1,0},{2,3},{3,2},{4,5},{5,4},{6,7},{7,6},{8,9},{9,8},{10,11... | collective-permute-start | bytes 2457608 | tf_op jit(solution)/shard_map/ppermute | solution.py:324
  211.7 18.7 %collective-permute-done.1 = bf16[640,640]{1,0:T(8,128)(2,1)} collective-permute-done((bf16[640,640]{1,0:T(8,128)(2,1)}, bf16[640,640]{1,0:T(8,128)(2,1)}, u32[]{:S(2)}, u32[]{:S(2)}) %collective-permute-start.1) | collective-permute-done | bytes 819232 | tf_op jit(solution)/shard_map/ppermute | solution.py:324
  230.3 0.0 copy-done.1
  230.3 0.0 copy-done.2
  230.3 2.6 %add_convert_fusion = bf16[640,640]{1,0:T(8,128)(2,1)} fusion(bf16[640,640]{1,0:T(8,128)(2,1)} %collective-permute-done.1, f32[640,1280]{1,0:T(8,128)S(1)} %fusion.1, s32[]{:T(128)S(6)} %select_n.39, bf16[640,640]{1,0:T(8,128)(2,1)} %param.14, f32[640]{0:T(1024)S(1)} %copy-done.1, f32[640]{0:T(1024)S(1)} %copy-done.2), kind=kLoop, calls=%fused_computation | loop fusion | flops 2867200 | bytes 4101124 | tf_op jit(solution)/shard_map/convert_element_type | solution.py:326
  (4 shorter events, 0.1 us)
Async XLA Ops:
  6.5 192.6 %all-gather.2.cloned.1.call-start = ((), (), s32[]{:S(2)}) async-start(), calls=%async_computation | async-start | bytes 4096000 | tf_op jit(solution)/shard_map/all_gather | solution.py:318
  72.0 1.1 copy-start
  137.6 12.0 %collective-permute-start = (bf16[2,640,128]{2,1,0:T(8,128)(2,1)S(1)}, bf16[2,640,128]{2,1,0:T(8,128)(2,1)S(1)}, u32[]{:S(2)}, u32[]{:S(2)}) collective-permute-start(bf16[2,640,128]{2,1,0:T(8,128)(2,1)S(1)} %slice.14), channel_id=1, source_target_pairs={{0,64},{8,72},{16,80},{24,88},{32,96},{40,104},{48,112},{56,120},{... | collective-permute-start | bytes 983048 | tf_op jit(solution)/shard_map/ppermute | solution.py:314
  199.1 31.2 %copy-start.1 = (f32[640]{0:T(1024)S(1)}, f32[640]{0:T(1024)}, u32[]{:S(2)}) copy-start(f32[640]{0:T(1024)} %param.13) | copy-start | bytes 7684
  199.1 31.2 %copy-start.2 = (f32[640]{0:T(1024)S(1)}, f32[640]{0:T(1024)}, u32[]{:S(2)}) copy-start(f32[640]{0:T(1024)} %param.15) | copy-start | bytes 7684
  208.5 21.8 %collective-permute-start.1 = (bf16[640,640]{1,0:T(8,128)(2,1)}, bf16[640,640]{1,0:T(8,128)(2,1)}, u32[]{:S(2)}, u32[]{:S(2)}) collective-permute-start(bf16[640,640]{1,0:T(8,128)(2,1)} %dynamic-slice_convert_fusion), channel_id=1, source_target_pairs={{0,1},{1,0},{2,3},{3,2},{4,5},{5,4},{6,7},{7,6},{8,9},{9,8},{10,11... | collective-permute-start | bytes 2457608 | tf_op jit(solution)/shard_map/ppermute | solution.py:324
Sparse Core Ops, SparseCore 0:
  151.6 47.4 all-gather.1

commit v2 on v1

--- a/solution.py
+++ b/solution.py
@@ -24,7 +24,7 @@
 
 def gather_kernel(
     q_ref, k_ref, v_ref, w_ref, kv_out, q_out, w_out,
-    stage, stage_sem, local_sem, send_sem, z_sem, x_sem, far_sem, sib_sem, w_sem, w_sib_sem,
+    stage, raw_values, stage_sem, local_sem, send_sem, z_sem, x_sem, far_sem, sib_sem, w_sem, w_sib_sem,
 ):
     zl, x, core, y, zh = place()
     other = 1 - zl
@@ -50,14 +50,24 @@
     def head_columns(h):
         return pl.ds(pl.multiple_of(h * HEAD_DIM, HEAD_DIM), HEAD_DIM)
 
-    staged = []
-    for plane, base in ((zl, 0), (other, 6)):
-        for j in range(2):
-            staged.append((k_ref, plane * 2 + j, base + 2 * j))
-            staged.append((v_ref, plane * 2 + j, base + 2 * j + 1))
-    staged += [(k_ref, 4, 4), (v_ref, 4, 5), (q_ref, other * 2, 10), (q_ref, other * 2 + 1, 11)]
+    own_a, pair_a = zl * 2, other * 2
+    staged = [
+        (k_ref, own_a, stage.at[0]),
+        (k_ref, own_a + 1, stage.at[2]),
+        (k_ref, 4, stage.at[4]),
+        (k_ref, pair_a, stage.at[6]),
+        (k_ref, pair_a + 1, stage.at[8]),
+        (q_ref, pair_a, stage.at[10]),
+        (q_ref, pair_a + 1, stage.at[11]),
+        (v_ref, own_a, raw_values.at[0]),
+        (v_ref, own_a + 1, raw_values.at[1]),
+        (v_ref, 4, raw_values.at[2]),
+        (v_ref, pair_a, raw_values.at[3]),
+        (v_ref, pair_a + 1, raw_values.at[4]),
+    ]
     stage_copies = [
-        pltpu.make_async_copy(src.at[:, head_columns(h)], stage.at[at], stage_sem.at[at]) for src, h, at in staged
+        pltpu.make_async_copy(src.at[:, head_columns(h)], dst, stage_sem.at[n])
+        for n, (src, h, dst) in enumerate(staged)
     ]
     for c in stage_copies:
         c.start()
@@ -77,6 +87,14 @@
         c.start()
     for c in stage_copies:
         c.wait()
+
+    def turn(n, _):
+        piece = lax.div(n, ROW_TILES)
+        rows = pl.ds(pl.multiple_of((n - piece * ROW_TILES) * TILE, TILE), TILE)
+        stage[2 * piece + 1, rows, :] = raw_values[piece, rows, :].T
+        return 0
+
+    lax.fori_loop(0, 5 * ROW_TILES, turn, 0)
     own = pltpu.make_async_copy(stage.at[pl.ds(0, 6)], kv_out.at[me], local_sem.at[4])
     own.start()
     pl.semaphore_wait(barrier, len(neighbours))
@@ -206,6 +224,7 @@
         out_specs=[pl.BlockSpec(memory_space=pl.ANY)] * 3,
         scratch_shapes=[
             pltpu.VMEM((12, ROWS, HEAD_DIM), bf16),
+            pltpu.VMEM((5, ROWS, HEAD_DIM), bf16),
             pltpu.SemaphoreType.DMA((12,)),
             pltpu.SemaphoreType.DMA((5,)),
             pltpu.SemaphoreType.DMA((64,)),
@@ -221,73 +240,260 @@
     )(q, k, v, w)
 
 
-GROUP = 4
-
-
-def attend_kernel(tiles_ref, counts_ref, q_ref, k_ref, v_ref, o_ref, scores):
-    j = pl.program_id(0)
-    scaling = HEAD_DIM ** -0.5
-
-    def one_row(i, _):
-        mine = i < ROW_TILES
-        slot = jnp.where(mine, j, 3 + j)
-        rows = pl.ds(pl.multiple_of(jnp.where(mine, i, i - ROW_TILES) * TILE, TILE), TILE)
-        q = q_ref[slot, rows, :]
-        count = counts_ref[i]
-        groups = lax.div(count + (GROUP - 1), GROUP)
-
-        def tile_of(ref, n):
-            t = tiles_ref[i, n]
-            owner = lax.div(t, ROW_TILES)
-            return ref[owner, 0, pl.ds(pl.multiple_of((t - owner * ROW_TILES) * TILE, TILE), TILE), :]
-
-        def score(g, peak):
-            keys = jnp.concatenate([tile_of(k_ref, g * GROUP + t) for t in range(GROUP)], axis=0)
-            s = lax.dot_general(q, keys, (((1,), (1,)), ((), ())), preferred_element_type=jnp.float32)
-            for t in range(GROUP):
-                part = jnp.where(g * GROUP + t < count, s[:, t * TILE : (t + 1) * TILE], MASKED)
-                scores[g * GROUP + t] = part
-                peak = jnp.maximum(peak, part)
-            return peak
-
-        peak = lax.fori_loop(0, groups, score, jnp.full((TILE, TILE), MASKED, jnp.float32))
-        row_max = jnp.max(peak, axis=1, keepdims=True)
-
-        def blend(g, carry):
-            total, acc = carry
-            values = jnp.concatenate([tile_of(v_ref, g * GROUP + t) for t in range(GROUP)], axis=0)
-            weights = [jnp.exp((scores[g * GROUP + t] - row_max) * scaling) for t in range(GROUP)]
-            for part in weights:
-                total = total + part
-            w = jnp.concatenate(weights, axis=1).astype(jnp.bfloat16)
-            return total, acc + jnp.dot(w, values, preferred_element_type=jnp.float32)
-
-        zero = jnp.zeros((TILE, HEAD_DIM), jnp.float32)
-        total, acc = lax.fori_loop(0, groups, blend, (zero, zero))
-        o_ref[slot, rows, :] = (acc / jnp.sum(total, axis=1, keepdims=True)).astype(o_ref.dtype)
-        return 0
-
-    lax.fori_loop(0, jnp.where(j < 2, 2 * ROW_TILES, ROW_TILES), one_row, 0)
+GROUP = 10
+LOG2E = 1.4426950408889634
+
+
+def attend_kernel(tiles_ref, counts_ref, q_ref, kv_hbm, o_ref, kv_ref, s00, s01, s02, s10, s11, s12, acc0, acc1, acc2, sem):
+    scores = ((s00, s01, s02), (s10, s11, s12))
+    accs = (acc0, acc1, acc2)
+    factor = HEAD_DIM ** -0.5 * LOG2E
+    loads = [pltpu.make_async_copy(kv_hbm.at[:, p], kv_ref.at[:, p], sem.at[p]) for p in (0, 2, 4, 1, 3, 5)]
+    for c in loads:
+        c.start()
+    for c in loads[:3]:
+        c.wait()
+
+    def place_of(row, n):
+        t = tiles_ref[row, n]
+        owner = lax.shift_right_logical(t * 205, 10)
+        return owner, pl.ds(pl.multiple_of((t - owner * ROW_TILES) * TILE, TILE), TILE)
+
+    def run(slots, base, between):
+        heads = len(slots)
+
+        def rows_of(i):
+            return pl.ds(pl.multiple_of(i * TILE, TILE), TILE)
+
+        def groups_of(i):
+            return lax.div(counts_ref[base + i] + (GROUP - 1), GROUP)
+
+        def load_queries(i):
+            qs = [q_ref[slot, rows_of(i), :].T for slot in slots]
+            zero = jnp.zeros((HEAD_DIM, TILE), jnp.bfloat16)
+            both = jnp.concatenate(
+                [jnp.concatenate([qs[0], zero], axis=1), jnp.concatenate([zero, qs[1]], axis=1)], axis=0
+            )
+            return [both] + qs[2:]
+
+        def score(i, side, g, peak, qt):
+            count = counts_ref[base + i]
+            at = [place_of(base + i, g * GROUP + t) for t in range(GROUP)]
+            keys = [jnp.concatenate([kv_ref[o, 2 * h, r, :] for o, r in at], axis=0) for h in range(heads)]
+            pair = jnp.dot(jnp.concatenate(keys[:2], axis=1), qt[0], preferred_element_type=jnp.float32)
+            s = [pair[:, :TILE], pair[:, TILE:]]
+            if heads == 3:
+                s.append(jnp.dot(keys[2], qt[1], preferred_element_type=jnp.float32))
+            out = []
+            for h in range(heads):
+                top = peak[h]
+                for t in range(GROUP):
+                    part = jnp.where(g * GROUP + t < count, s[h][t * TILE : (t + 1) * TILE], MASKED)
+                    scores[side][h][g * GROUP + t] = part
+                    top = jnp.maximum(top, jnp.max(part.reshape(TILE // 8, 8, TILE), axis=0))
+                out.append(top)
+            return tuple(out)
+
+        def blend(i, side, g, totals, peak):
+            at = [place_of(base + i, g * GROUP + t) for t in range(GROUP)]
+            out = []
+            for h in range(heads):
+                total = totals[h]
+                weights = []
+                for t in range(GROUP):
+                    w = jnp.exp2((scores[side][h][g * GROUP + t] - peak[h]) * factor)
+                    total = total + jnp.sum(w.reshape(TILE // 8, 8, TILE), axis=0)
+                    weights.append(w.astype(jnp.bfloat16))
+                values = jnp.concatenate([kv_ref[o, 2 * h + 1, r, :] for o, r in at], axis=1)
+                accs[h][...] += jnp.dot(values, jnp.concatenate(weights, axis=0), preferred_element_type=jnp.float32)
+                out.append(total)
+            return tuple(out)
+
+        lowest = tuple(jnp.full((8, TILE), MASKED, jnp.float32) for _ in slots)
+        zeros = tuple(jnp.zeros((8, TILE), jnp.float32) for _ in slots)
+
+        def row_max(peak):
+            return tuple(jnp.max(p, axis=0, keepdims=True) for p in peak)
+
+        def clear():
+            for h in range(heads):
+                accs[h][...] = jnp.zeros((HEAD_DIM, TILE), jnp.float32)
+
+        def finish(i, totals):
+            for h in range(heads):
+                o = accs[h][...] * (1.0 / jnp.sum(totals[h], axis=0, keepdims=True))
+                o_ref[slots[h], rows_of(i), :] = o.T.astype(o_ref.dtype)
+
+        def step(i, side, peak):
+            qt = load_queries(i + 1)
+            peak = row_max(peak)
+            clear()
+            here, there = groups_of(i), groups_of(i + 1)
+            both = jnp.minimum(here, there)
+
+            def together(g, carry):
+                return score(i + 1, 1 - side, g, carry[0], qt), blend(i, side, g, carry[1], peak)
+
+            above, totals = lax.fori_loop(0, both, together, (lowest, zeros))
+            above = lax.fori_loop(both, there, lambda g, c: score(i + 1, 1 - side, g, c, qt), above)
+            totals = lax.fori_loop(both, here, lambda g, c: blend(i, side, g, c, peak), totals)
+            finish(i, totals)
+            return above
+
+        qt = load_queries(0)
+        peak = lax.fori_loop(0, groups_of(0), lambda g, c: score(0, 0, g, c, qt), lowest)
+        between()
+        peak = lax.fori_loop(0, 2, lambda n, c: step(2 * n + 1, 1, step(2 * n, 0, c)), peak)
+        peak = row_max(peak)
+        clear()
+        finish(4, lax.fori_loop(0, groups_of(4), lambda g, c: blend(4, 0, g, c, peak), zeros))
+
+    def values_here():
+        for c in loads[3:]:
+            c.wait()
+
+    run((0, 1, 2), 0, values_here)
+    run((3, 4), ROW_TILES, lambda: None)
 
 
 def attend(tiles, counts, q, kv):
+    room = -(-TILE_COUNT // GROUP) * GROUP
     return pl.pallas_call(
         attend_kernel,
         out_shape=jax.ShapeDtypeStruct((5, ROWS, HEAD_DIM), jnp.bfloat16),
-        grid_spec=pltpu.PrefetchScalarGridSpec(
-            num_scalar_prefetch=2,
-            grid=(3,),
-            in_specs=[
-                pl.BlockSpec((5, ROWS, HEAD_DIM), lambda j, *_: (0, 0, 0)),
-                pl.BlockSpec((SEQ, 1, ROWS, HEAD_DIM), lambda j, *_: (0, 2 * j, 0, 0)),
-                pl.BlockSpec((SEQ, 1, ROWS, HEAD_DIM), lambda j, *_: (0, 2 * j + 1, 0, 0)),
-            ],
-            out_specs=pl.BlockSpec((5, ROWS, HEAD_DIM), lambda j, *_: (0, 0, 0)),
-            scratch_shapes=[pltpu.VMEM((TILE_COUNT, TILE, TILE), jnp.float32)],
-        ),
-        compiler_params=pltpu.CompilerParams(vmem_limit_bytes=48 << 20),
+        in_specs=[pl.BlockSpec(memory_space=pltpu.SMEM)] * 2
+        + [pl.BlockSpec(memory_space=pltpu.VMEM), pl.BlockSpec(memory_space=pl.ANY)],
+        out_specs=pl.BlockSpec(memory_space=pltpu.VMEM),
+        scratch_shapes=[pltpu.VMEM((SEQ, 6, ROWS, HEAD_DIM), jnp.bfloat16)]
+        + [pltpu.VMEM((room, TILE, TILE), jnp.float32)] * 6
+        + [pltpu.VMEM((HEAD_DIM, TILE), jnp.float32)] * 3
+        + [pltpu.SemaphoreType.DMA((6,))],
+        compiler_params=pltpu.CompilerParams(vmem_limit_bytes=60 << 20),
         name="attend",
-    )(tiles, counts, q, kv, kv)
+    )(tiles, counts, q, kv)
+
+
+def project_kernel(
+    o_ref, w_hbm, bias_ref, gate_ref, res_ref, out_ref,
+    w, att, mine, sent, got, w_sem, put_sem, send_sem, z_sem, y_sem, far_sem, sum_sem,
+):
+    zl, x, core, y, zh = place()
+    other = 1 - zl
+    me = (zl * RING + x) * 2 + core
+    head_me = y * 2 + zh
+    to_pair = ((other * RING + x) * 2 + core, head_me)
+    right, left, opposite = lax.rem(y + 1, RING), lax.rem(y + 3, RING), lax.rem(y + 2, RING)
+    to_right, to_left = (me, right * 2 + zh), (me, left * 2 + zh)
+    to_sum = (me, y * 2 + 1 - zh)
+
+    barrier = pltpu.get_barrier_semaphore()
+    neighbours = [to_pair, to_right, to_left, to_sum]
+    for n in neighbours:
+        pl.semaphore_signal(barrier, inc=1, device_id=n, device_id_type=MESH)
+    fetch = pltpu.make_async_copy(w_hbm, w, w_sem)
+    fetch.start()
+    puts = []
+    for c in range(ROW_TILES):
+        rows = pl.ds(c * TILE, TILE)
+        puts.append(
+            pltpu.make_async_copy(o_ref.at[pl.ds(0, 2), rows], att.at[c, y, pl.ds(2 * zl, 2)], put_sem.at[2 * c])
+        )
+        puts.append(pltpu.make_async_copy(o_ref.at[2, rows], att.at[c, y, 4], put_sem.at[2 * c + 1]))
+    for c in puts:
+        c.start()
+    pl.semaphore_wait(barrier, len(neighbours))
+
+    sends = []
+
+    def send(src, dst, recv, target):
+        c = pltpu.make_async_remote_copy(
+            src_ref=src, dst_ref=dst, send_sem=send_sem.at[len(sends)], recv_sem=recv, device_id=target, device_id_type=MESH
+        )
+        c.start()
+        sends.append(c)
+
+    def arrived(dst, recv, source):
+        pltpu.make_async_remote_copy(
+            src_ref=dst, dst_ref=dst, send_sem=send_sem.at[0], recv_sem=recv, device_id=source, device_id_type=MESH
+        ).wait_recv()
+
+    for c in range(ROW_TILES):
+        send(
+            o_ref.at[pl.ds(3, 2), pl.ds(c * TILE, TILE)], att.at[c, y, pl.ds(2 * zl, 2)], z_sem.at[c], to_pair
+        )
+    for c in range(ROW_TILES):
+        puts[2 * c].wait()
+        puts[2 * c + 1].wait()
+        arrived(att.at[c, y, pl.ds(2 * other, 2)], z_sem.at[c], to_pair)
+        send(att.at[c, y], att.at[c, y], y_sem.at[0, c], to_right)
+        send(att.at[c, y], att.at[c, y], y_sem.at[1, c], to_left)
+
+    def halves(c):
+        cut = 3 if c % 2 == 0 else 2
+        return pl.ds(0, cut), pl.ds(cut, 5 - cut)
+
+    def contract(c):
+        first, second = halves(c)
+        arrived(att.at[c, opposite, first], far_sem.at[0, c], to_left)
+        arrived(att.at[c, opposite, second], far_sem.at[1, c], to_right)
+        if c == 0:
+            fetch.wait()
+        rows = jnp.concatenate([att[c, n, h] for n in range(RING) for h in range(5)], axis=1)
+        theirs = w[:, pl.ds(pl.multiple_of((1 - zh) * ROWS, TILE), ROWS)]
+        sent[c] = jnp.dot(rows, theirs, preferred_element_type=jnp.float32).astype(jnp.bfloat16)
+        send(sent.at[c], got.at[c], sum_sem.at[c], to_sum)
+        ours = w[:, pl.ds(pl.multiple_of(zh * ROWS, TILE), ROWS)]
+        mine[c] = jnp.dot(rows, ours, preferred_element_type=jnp.float32)
+
+    for c in range(ROW_TILES):
+        first, second = halves(c)
+        arrived(att.at[c, left], y_sem.at[0, c], to_left)
+        send(att.at[c, left, first], att.at[c, left, first], far_sem.at[0, c], to_right)
+        arrived(att.at[c, right], y_sem.at[1, c], to_right)
+        send(att.at[c, right, second], att.at[c, right, second], far_sem.at[1, c], to_left)
+        if c > 0:
+            contract(c - 1)
+    contract(ROW_TILES - 1)
+    for c in range(ROW_TILES):
+        arrived(got.at[c], sum_sem.at[c], to_sum)
+        rows = pl.ds(c * TILE, TILE)
+        projected = mine[c] + got[c].astype(jnp.float32)
+        out = res_ref[rows, :].astype(jnp.float32) + gate_ref[...] * (projected + bias_ref[...])
+        out_ref[rows, :] = out.astype(out_ref.dtype)
+    for c in sends:
+        c.wait_send()
+
+
+def project(o, panel, bias, gate, residual):
+    bf16 = jnp.bfloat16
+    return pl.pallas_call(
+        project_kernel,
+        out_shape=jax.ShapeDtypeStruct((ROWS, ROWS), bf16),
+        in_specs=[
+            pl.BlockSpec(memory_space=pltpu.VMEM),
+            pl.BlockSpec(memory_space=pl.ANY),
+            pl.BlockSpec(memory_space=pltpu.VMEM),
+            pl.BlockSpec(memory_space=pltpu.VMEM),
+            pl.BlockSpec(memory_space=pltpu.VMEM),
+        ],
+        out_specs=pl.BlockSpec(memory_space=pltpu.VMEM),
+        scratch_shapes=[
+            pltpu.VMEM((RING * ROWS, 2 * ROWS), bf16),
+            pltpu.VMEM((ROW_TILES, RING, 5, TILE, HEAD_DIM), bf16),
+            pltpu.VMEM((ROW_TILES, TILE, ROWS), jnp.float32),
+            pltpu.VMEM((ROW_TILES, TILE, ROWS), bf16),
+            pltpu.VMEM((ROW_TILES, TILE, ROWS), bf16),
+            pltpu.SemaphoreType.DMA,
+            pltpu.SemaphoreType.DMA((10,)),
+            pltpu.SemaphoreType.DMA((32,)),
+            pltpu.SemaphoreType.DMA((5,)),
+            pltpu.SemaphoreType.DMA((2, 5)),
+            pltpu.SemaphoreType.DMA((2, 5)),
+            pltpu.SemaphoreType.DMA((5,)),
+        ],
+        compiler_params=pltpu.CompilerParams(collective_id=1, has_side_effects=True, vmem_limit_bytes=40 << 20),
+        name="project",
+    )(o, panel, bias, gate, residual)
 
 
 def tile_lists(tile_mask):
@@ -306,24 +512,10 @@
 
 
 def local(queries, key_states, value_states, tile_mask, out_weight, out_bias, residual, gate_scale):
-    zl, x, core, y, zh = place()
     tiles, counts = tile_lists(tile_mask)
     kv, q, panel = gather(queries, key_states, value_states, out_weight)
     o = attend(tiles, counts, q, kv)
-    pairs = [(s, (s + 8) % 16) for s in range(SEQ)]
-    back = lax.ppermute(o[3:5], "seq", pairs)
-    low = jnp.where(zl == 0, o[0:2], back)
-    high = jnp.where(zl == 0, back, o[0:2])
-    attended = jnp.concatenate([low, high, o[2:3]], axis=0).transpose(1, 0, 2).reshape(ROWS, ROWS)
-    gathered = lax.all_gather(
-        attended, "head", axis=1, tiled=True, axis_index_groups=[[0, 2, 4, 6], [1, 3, 5, 7]]
-    )
-    partial = jnp.dot(gathered, panel.reshape(RING * ROWS, 2 * ROWS), preferred_element_type=jnp.float32)
-    mine = lax.dynamic_slice_in_dim(partial, zh * ROWS, ROWS, 1)
-    theirs = lax.dynamic_slice_in_dim(partial, (1 - zh) * ROWS, ROWS, 1).astype(jnp.bfloat16)
-    projected = mine + lax.ppermute(theirs, "head", [(h, h ^ 1) for h in range(8)]).astype(jnp.float32)
-    result = residual.astype(jnp.float32) + gate_scale[None, :] * (projected + out_bias[None, :])
-    return result.astype(jnp.bfloat16)
+    return project(o, panel.reshape(RING * ROWS, 2 * ROWS), out_bias[None, :], gate_scale[None, :], residual)
 
 
 def solution(mesh):

time: 240 us -> 152 us (0.63)
  the two profiles are of different devices: /device:TPU:0 before, /device:TPU:4 now
where the time goes in v2:
time: 152 us; the launch traced here: 151 us
  Pallas kernels  144 us (95%)
  local copies, waits for them, and re-layouts  5.64 us (4%)
  other arithmetic  1.81 us (1%)
    pallas_call x1, Pallas kernels, gather(): pl.pallas_call(gather_kernel, out_shape=[jax.ShapeDtypeStruct((SEQ, 6, RO...  62.3 us
    pallas_call x1, Pallas kernels, project(): pl.pallas_call(project_kernel, out_shape=jax.ShapeDtypeStruct((ROWS, ROWS...  52.4 us
    pallas_call x1, Pallas kernels, attend(): pl.pallas_call(attend_kernel, out_shape=jax.ShapeDtypeStruct((5, ROWS, HE...  29 us
    unnamed x11, local copies, waits for them, and re-layouts  4.91 us

profile of v2, /device:TPU:4, one launch (start us, length us, event | category | flops | bytes accessed | tf_op | source)
XLA Modules:
  0.0 151.3 jit_solution(13036762989966282412)
XLA Ops:
  0.0 0.7 constant_dynamic-slice_fusion.1
  0.7 0.7 convert_reduce_fusion
  1.4 0.3 select_reduce_fusion.1
  1.7 0.9 select_reduce_fusion.tiles_ref
  2.5 62.3 %gather_heads.1 = (bf16[16,6,640,128]{3,2,1,0:T(8,128)(2,1)}, bf16[5,640,128]{2,1,0:T(8,128)(2,1)}, bf16[4,640,1280]{2,1,0:T(8,128)(2,1)}) custom-call(bf16[640,640]{1,0:T(8,128)(2,1)} %q_ref.1, bf16[640,640]{1,0:T(8,128)(2,1)} %k_ref.1, bf16[640,640]{1,0:T(8,128)(2,1)} %v_ref.1, bf16[640,5120]{1,0:T(8,128)(2,1)} %w_ref.1), custom_call_target="tpu_custom_call" | custom-call | tf_op jit(solution)/shard_map/gather_heads/pallas_call | solution.py:216
  64.9 0.0 copy-start.3
  64.9 0.0 copy-start.4
  64.9 0.0 copy-start.2
  64.9 29.0 %attend.1.o_ref = bf16[5,640,128]{2,1,0:T(8,128)(2,1)} custom-call(s32[10,80]{1,0:T(8,128)} %select_reduce_fusion.tiles_ref, s32[10]{0:T(128)} %get-tuple-element.11.counts_ref, bf16[5,640,128]{2,1,0:T(8,128)(2,1)} %get-tuple-element.8.q_ref, bf16[16,6,640,128]{3,2,1,0:T(8,128)(2,1)} %get-tuple-element.9.kv_hbm), custom_call_target="tpu_custom_call" | custom-call | tf_op jit(solution)/shard_map/attend/pallas_call | solution.py:361
  93.9 0.0 copy-done.3
  93.9 0.0 copy-done.4
  94.0 0.0 copy-done.2
  94.0 0.0 copy-start
  94.0 2.9 %copy-done = bf16[4,640,1280]{2,1,0:T(8,128)(2,1)S(1)} copy-done((bf16[4,640,1280]{2,1,0:T(8,128)(2,1)S(1)}, bf16[4,640,1280]{2,1,0:T(8,128)(2,1)}, u32[]{:S(2)}) %copy-start) | copy-done | bytes 6553624
  96.8 0.0 copy-start.1
  96.8 1.1 copy-done.1
  98.0 52.4 %project.1 = bf16[640,640]{1,0:T(8,128)(2,1)S(1)} custom-call(bf16[5,640,128]{2,1,0:T(8,128)(2,1)S(1)} %copy-done.1, bf16[2560,1280]{1,0:T(8,128)(2,1)S(1)} %bitcast.1, f32[1,640]{1,0:T(1,128)S(1)} %broadcast_in_dim.34.bias_ref, f32[1,640]{1,0:T(1,128)S(1)} %broadcast_in_dim.35.gate_ref, bf16[640,640]{1,0:T(8,128)(2,1)S(1)} %copy-done.2), custom_call_target="tpu_custom_call" | custom-call | tf_op jit(solution)/shard_map/project/pallas_call | solution.py:469
  150.4 0.9 copy.10
  (3 shorter events, 0.0 us)
Async XLA Ops:
  64.9 29.0 %copy-start.3 = (f32[640]{0:T(1024)S(1)}, f32[640]{0:T(1024)}, u32[]{:S(2)}) copy-start(f32[640]{0:T(1024)} %param.13) | copy-start | bytes 7684
  64.9 29.1 %copy-start.4 = (f32[640]{0:T(1024)S(1)}, f32[640]{0:T(1024)}, u32[]{:S(2)}) copy-start(f32[640]{0:T(1024)} %param.15) | copy-start | bytes 7684
  64.9 29.1 %copy-start.2 = (bf16[640,640]{1,0:T(8,128)(2,1)S(1)}, bf16[640,640]{1,0:T(8,128)(2,1)}, u32[]{:S(2)}) copy-start(bf16[640,640]{1,0:T(8,128)(2,1)} %res_ref.1) | copy-start | bytes 2457604
  94.0 2.9 %copy-start = (bf16[4,640,1280]{2,1,0:T(8,128)(2,1)S(1)}, bf16[4,640,1280]{2,1,0:T(8,128)(2,1)}, u32[]{:S(2)}) copy-start(bf16[4,640,1280]{2,1,0:T(8,128)(2,1)} %get-tuple-element.10) | copy-start | bytes 19660804
  96.8 1.1 copy-start.1

commit v3 on v2

--- a/solution.py
+++ b/solution.py
@@ -244,13 +244,31 @@
 LOG2E = 1.4426950408889634
 
 
-def attend_kernel(tiles_ref, counts_ref, q_ref, kv_hbm, o_ref, kv_ref, s00, s01, s02, s10, s11, s12, acc0, acc1, acc2, sem):
+def attend_kernel(
+    mask_ref, q_ref, kv_hbm, o_ref, tiles_ref, counts_ref, kv_ref, s00, s01, s02, s10, s11, s12, acc0, acc1, acc2, sem
+):
     scores = ((s00, s01, s02), (s10, s11, s12))
     accs = (acc0, acc1, acc2)
     factor = HEAD_DIM ** -0.5 * LOG2E
     loads = [pltpu.make_async_copy(kv_hbm.at[:, p], kv_ref.at[:, p], sem.at[p]) for p in (0, 2, 4, 1, 3, 5)]
     for c in loads:
         c.start()
+    zl, x, core, _, _ = place()
+    first = ((zl * RING + x) * 2 + core) * ROW_TILES
+    first_pair = (((1 - zl) * RING + x) * 2 + core) * ROW_TILES
+
+    def compact(i, _):
+        row = jnp.where(i < ROW_TILES, first + i, first_pair + i - ROW_TILES)
+        count = jnp.int32(0)
+        for t in range(TILE_COUNT):
+            tiles_ref[i, count] = jnp.int32(t)
+            count = count + jnp.where(mask_ref[row, t] > 0, 1, 0)
+        for t in range(GROUP):
+            tiles_ref[i, count + t] = jnp.int32(0)
+        counts_ref[i] = count
+        return 0
+
+    lax.fori_loop(0, 2 * ROW_TILES, compact, 0)
     for c in loads[:3]:
         c.wait()
 
@@ -356,26 +374,33 @@
     run((3, 4), ROW_TILES, lambda: None)
 
 
-def attend(tiles, counts, q, kv):
+def attend(tile_mask, q, kv):
     room = -(-TILE_COUNT // GROUP) * GROUP
     return pl.pallas_call(
         attend_kernel,
         out_shape=jax.ShapeDtypeStruct((5, ROWS, HEAD_DIM), jnp.bfloat16),
-        in_specs=[pl.BlockSpec(memory_space=pltpu.SMEM)] * 2
-        + [pl.BlockSpec(memory_space=pltpu.VMEM), pl.BlockSpec(memory_space=pl.ANY)],
+        in_specs=[
+            pl.BlockSpec(memory_space=pltpu.SMEM),
+            pl.BlockSpec(memory_space=pltpu.VMEM),
+            pl.BlockSpec(memory_space=pl.ANY),
+        ],
         out_specs=pl.BlockSpec(memory_space=pltpu.VMEM),
-        scratch_shapes=[pltpu.VMEM((SEQ, 6, ROWS, HEAD_DIM), jnp.bfloat16)]
+        scratch_shapes=[
+            pltpu.SMEM((2 * ROW_TILES, TILE_COUNT + 16), jnp.int32),
+            pltpu.SMEM((2 * ROW_TILES,), jnp.int32),
+            pltpu.VMEM((SEQ, 6, ROWS, HEAD_DIM), jnp.bfloat16),
+        ]
         + [pltpu.VMEM((room, TILE, TILE), jnp.float32)] * 6
         + [pltpu.VMEM((HEAD_DIM, TILE), jnp.float32)] * 3
         + [pltpu.SemaphoreType.DMA((6,))],
         compiler_params=pltpu.CompilerParams(vmem_limit_bytes=60 << 20),
         name="attend",
-    )(tiles, counts, q, kv)
+    )(tile_mask, q, kv)
 
 
 def project_kernel(
-    o_ref, w_hbm, bias_ref, gate_ref, res_ref, out_ref,
-    w, att, mine, sent, got, w_sem, put_sem, send_sem, z_sem, y_sem, far_sem, sum_sem,
+    o_ref, w_hbm, bias_ref, gate_ref, res_hbm, out_ref,
+    w, res_ref, att, mine, sent, got, w_sem, res_sem, put_sem, send_sem, z_sem, y_sem, far_sem, sum_sem,
 ):
     zl, x, core, y, zh = place()
     other = 1 - zl
@@ -392,6 +417,8 @@
         pl.semaphore_signal(barrier, inc=1, device_id=n, device_id_type=MESH)
     fetch = pltpu.make_async_copy(w_hbm, w, w_sem)
     fetch.start()
+    fetch_res = pltpu.make_async_copy(res_hbm, res_ref, res_sem)
+    fetch_res.start()
     puts = []
     for c in range(ROW_TILES):
         rows = pl.ds(c * TILE, TILE)
@@ -454,6 +481,7 @@
         if c > 0:
             contract(c - 1)
     contract(ROW_TILES - 1)
+    fetch_res.wait()
     for c in range(ROW_TILES):
         arrived(got.at[c], sum_sem.at[c], to_sum)
         rows = pl.ds(c * TILE, TILE)
@@ -474,15 +502,17 @@
             pl.BlockSpec(memory_space=pl.ANY),
             pl.BlockSpec(memory_space=pltpu.VMEM),
             pl.BlockSpec(memory_space=pltpu.VMEM),
-            pl.BlockSpec(memory_space=pltpu.VMEM),
+            pl.BlockSpec(memory_space=pl.ANY),
         ],
         out_specs=pl.BlockSpec(memory_space=pltpu.VMEM),
         scratch_shapes=[
             pltpu.VMEM((RING * ROWS, 2 * ROWS), bf16),
+            pltpu.VMEM((ROWS, ROWS), bf16),
             pltpu.VMEM((ROW_TILES, RING, 5, TILE, HEAD_DIM), bf16),
             pltpu.VMEM((ROW_TILES, TILE, ROWS), jnp.float32),
             pltpu.VMEM((ROW_TILES, TILE, ROWS), bf16),
             pltpu.VMEM((ROW_TILES, TILE, ROWS), bf16),
+            pltpu.SemaphoreType.DMA,
             pltpu.SemaphoreType.DMA,
             pltpu.SemaphoreType.DMA((10,)),
             pltpu.SemaphoreType.DMA((32,)),
@@ -491,9 +521,444 @@
             pltpu.SemaphoreType.DMA((2, 5)),
             pltpu.SemaphoreType.DMA((5,)),
         ],
-        compiler_params=pltpu.CompilerParams(collective_id=1, has_side_effects=True, vmem_limit_bytes=40 << 20),
+        compiler_params=pltpu.CompilerParams(collective_id=1, has_side_effects=True, vmem_limit_bytes=62 << 20),
         name="project",
     )(o, panel, bias, gate, residual)
+
+
+LIMIT = 40
+STEPS = LIMIT // GROUP
+KEYS_OF = pl.ds(0, 1)
+VALUES_OF = pl.ds(1, 1)
+
+
+def whole_kernel(
+    owners_ref, starts_ref, bars_ref, q_ref, k_ref, v_ref, w_ref, bias_ref, gate_ref, res_hbm, out_ref,
+    stage, raw_values, kva, kvb, kvh, q_own, q_pair, att, back, panel, mine, theirs, sent, got, res_ref,
+    s00, s01, s10, s11, acc0, acc1,
+    stage_sem, local_sem, send_sem, z_sem, x_sem, far_sem, sib_sem, w_sem, w_sib_sem, ret_sem, y_sem, y_far_sem, sum_sem,
+):
+    zl, x, core, y, zh = place()
+    other = 1 - zl
+    right, left, opposite = lax.rem(x + 1, RING), lax.rem(x + 3, RING), lax.rem(x + 2, RING)
+    y_right, y_left, y_opposite = lax.rem(y + 1, RING), lax.rem(y + 3, RING), lax.rem(y + 2, RING)
+
+    def seq_of(zl_, x_, core_):
+        return (zl_ * RING + x_) * 2 + core_
+
+    head_me = y * 2 + zh
+    me = seq_of(zl, x, core)
+    to_pair = (seq_of(other, x, core), head_me)
+    to_right = (seq_of(zl, right, core), head_me)
+    to_left = (seq_of(zl, left, core), head_me)
+    to_sib = (seq_of(zl, x, 1 - core), head_me)
+    to_y = [(me, lax.rem(y + d, RING) * 2 + zh) for d in (1, 2, 3)]
+    to_sum = (me, y * 2 + 1 - zh)
+
+    barrier = pltpu.get_barrier_semaphore()
+    neighbours = [to_pair, to_right, to_left, to_sib, to_sum] + to_y
+    for n in neighbours:
+        pl.semaphore_signal(barrier, inc=1, device_id=n, device_id_type=MESH)
+
+    def head_columns(h):
+        return pl.ds(pl.multiple_of(h * HEAD_DIM, HEAD_DIM), HEAD_DIM)
+
+    own_a, pair_a = zl * 2, other * 2
+    staged = [
+        (k_ref, pair_a, stage.at[6]),
+        (v_ref, pair_a, raw_values.at[3]),
+        (k_ref, own_a, stage.at[0]),
+        (v_ref, own_a, raw_values.at[0]),
+        (k_ref, own_a + 1, stage.at[2]),
+        (v_ref, own_a + 1, raw_values.at[1]),
+        (k_ref, pair_a + 1, stage.at[8]),
+        (v_ref, pair_a + 1, raw_values.at[4]),
+        (k_ref, 4, stage.at[4]),
+        (v_ref, 4, raw_values.at[2]),
+        (q_ref, pair_a, stage.at[10]),
+        (q_ref, pair_a + 1, stage.at[11]),
+    ]
+    stage_copies = [
+        pltpu.make_async_copy(src.at[:, :, head_columns(h)], dst, stage_sem.at[n])
+        for n, (src, h, dst) in enumerate(staged)
+    ]
+    for c in stage_copies:
+        c.start()
+    half = pl.ds(pl.multiple_of(core * (ROWS // 2), ROWS // 2), ROWS // 2)
+    other_half = pl.ds(pl.multiple_of((1 - core) * (ROWS // 2), ROWS // 2), ROWS // 2)
+
+    def columns_of(y_):
+        return pl.ds(pl.multiple_of(y_ * (2 * ROWS), 2 * ROWS), 2 * ROWS)
+
+    local = [
+        pltpu.make_async_copy(q_ref.at[:, :, head_columns(own_a)], q_own.at[0], local_sem.at[0]),
+        pltpu.make_async_copy(q_ref.at[:, :, head_columns(own_a + 1)], q_own.at[1], local_sem.at[1]),
+        pltpu.make_async_copy(q_ref.at[:, :, head_columns(4)], q_own.at[2], local_sem.at[2]),
+        pltpu.make_async_copy(w_ref.at[half, columns_of(y)], panel.at[y, half], local_sem.at[3]),
+        pltpu.make_async_copy(res_hbm, res_ref, local_sem.at[4]),
+    ]
+    for c in local:
+        c.start()
+    for c in stage_copies:
+        c.wait()
+
+    def turn(n, _):
+        piece = lax.div(n, ROW_TILES)
+        r = n - piece * ROW_TILES
+        stage[2 * piece + 1, r] = raw_values[piece, r].T
+        return 0
+
+    lax.fori_loop(0, 5 * ROW_TILES, turn, 0)
+    own = [
+        pltpu.make_async_copy(stage.at[pl.ds(2 * n, 2)], kv.at[me], local_sem.at[5 + n])
+        for n, kv in enumerate((kva, kvb, kvh))
+    ]
+    for c in own:
+        c.start()
+    pl.semaphore_wait(barrier, len(neighbours))
+
+    sends = []
+
+    def send(src, dst, recv, target):
+        c = pltpu.make_async_remote_copy(
+            src_ref=src, dst_ref=dst, send_sem=send_sem.at[len(sends)], recv_sem=recv, device_id=target, device_id_type=MESH
+        )
+        c.start()
+        sends.append(c)
+
+    def arrived(dst, recv, source):
+        pltpu.make_async_remote_copy(
+            src_ref=dst, dst_ref=dst, send_sem=send_sem.at[0], recv_sem=recv, device_id=source, device_id_type=MESH
+        ).wait_recv()
+
+    both_parts = pl.ds(0, 2)
+    k_part, v_part = KEYS_OF, VALUES_OF
+    sib_waits = {"a": [], "b": [], "h": []}
+    sib_count = [0]
+
+    def block(kv, zl_, x_, part=both_parts):
+        return kv.at[seq_of(zl_, x_, core), part]
+
+    def to_sibling(name, kv, zl_, x_, part=both_parts):
+        n = sib_count[0]
+        sib_count[0] += 1
+        send(block(kv, zl_, x_, part), block(kv, zl_, x_, part), sib_sem.at[n], to_sib)
+        sib_waits[name].append((n, kv, zl_, x_, part))
+
+    def from_sibling(name):
+        for n, kv, zl_, x_, part in sib_waits[name]:
+            arrived(kv.at[seq_of(zl_, x_, 1 - core), part], sib_sem.at[n], to_sib)
+
+    def ring_send(item, kv, zl_, x_, part=both_parts):
+        send(block(kv, zl_, x_, part), block(kv, zl_, x_, part), x_sem.at[0, item], to_right)
+        send(block(kv, zl_, x_, part), block(kv, zl_, x_, part), x_sem.at[1, item], to_left)
+
+    def ring_pass(item, name, kv, zl_):
+        arrived(block(kv, zl_, left), x_sem.at[0, item], to_left)
+        send(block(kv, zl_, left, k_part), block(kv, zl_, left, k_part), far_sem.at[0, item], to_right)
+        arrived(block(kv, zl_, right), x_sem.at[1, item], to_right)
+        send(block(kv, zl_, right, v_part), block(kv, zl_, right, v_part), far_sem.at[1, item], to_left)
+        to_sibling(name, kv, zl_, left)
+        to_sibling(name, kv, zl_, right)
+
+    def ring_far(item, name, kv, zl_):
+        arrived(block(kv, zl_, opposite, k_part), far_sem.at[0, item], to_left)
+        arrived(block(kv, zl_, opposite, v_part), far_sem.at[1, item], to_right)
+        to_sibling(name, kv, zl_, opposite)
+
+    A0, A1, B0, B1, H0, V1 = range(6)
+    send(stage.at[pl.ds(6, 2)], kva.at[me], z_sem.at[0], to_pair)
+    own[0].wait()
+    ring_send(A0, kva, zl, x)
+    to_sibling("a", kva, zl, x)
+    for d in range(3):
+        send(w_ref.at[half, columns_of(lax.rem(y + d + 1, RING))], panel.at[y, half], w_sem.at[d], to_y[d])
+    own[1].wait()
+    own[2].wait()
+    arrived(block(kva, other, x), z_sem.at[0], to_pair)
+    ring_send(A1, kva, other, x)
+    send(stage.at[pl.ds(8, 2)], kvb.at[me], z_sem.at[1], to_pair)
+    send(stage.at[pl.ds(10, 2)], q_pair, z_sem.at[2], to_pair)
+    to_sibling("a", kva, other, x)
+    ring_pass(A0, "a", kva, zl)
+    ring_pass(A1, "a", kva, other)
+    ring_send(B0, kvb, zl, x)
+    to_sibling("b", kvb, zl, x)
+    arrived(block(kvb, other, x), z_sem.at[1], to_pair)
+    ring_send(B1, kvb, other, x)
+    to_sibling("b", kvb, other, x)
+    send(stage.at[pl.ds(4, 2)], kvh.at[me], z_sem.at[3], to_pair)
+    ring_far(A0, "a", kva, zl)
+    ring_far(A1, "a", kva, other)
+    for c in local[:3]:
+        c.wait()
+    arrived(q_pair, z_sem.at[2], to_pair)
+    from_sibling("a")
+
+    scores = ((s00, s01), (s10, s11))
+    accs = (acc0, acc1)
+    factor = HEAD_DIM ** -0.5 * LOG2E
+    lowest = jnp.full((8, TILE), MASKED, jnp.float32)
+    nothing = jnp.zeros((8, TILE), jnp.float32)
+
+    def place_of(row, n):
+        return owners_ref[row, n], starts_ref[row, n]
+
+    def score(kv, rows, side, g, peaks, queries):
+        out = []
+        for u, row in enumerate(rows):
+            at = [place_of(row, g * GROUP + t) for t in range(GROUP)]
+            keys = jnp.concatenate([kv[o, 0, r] for o, r in at], axis=0)
+            s = jnp.dot(keys, queries[u], preferred_element_type=jnp.float32)
+            top = peaks[u]
+            for t in range(GROUP):
+                part = s[t * TILE : (t + 1) * TILE] + bars_ref[row, g * GROUP + t]
+                scores[side][u][g * GROUP + t] = part
+                top = jnp.maximum(top, jnp.max(part.reshape(TILE // 8, 8, TILE), axis=0))
+            out.append(top)
+        return tuple(out)
+
+    def blend(kv, rows, side, g, totals, peaks):
+        out = []
+        for u, row in enumerate(rows):
+            total = totals[u]
+            weights = []
+            for t in range(GROUP):
+                w = jnp.exp2((scores[side][u][g * GROUP + t] - peaks[u]) * factor)
+                total = total + jnp.sum(w.reshape(TILE // 8, 8, TILE), axis=0)
+                weights.append(w.astype(jnp.bfloat16))
+            at = [place_of(row, g * GROUP + t) for t in range(GROUP)]
+            values = jnp.concatenate([kv[o, 1, r] for o, r in at], axis=1)
+            accs[u][...] += jnp.dot(values, jnp.concatenate(weights, axis=0), preferred_element_type=jnp.float32)
+            out.append(total)
+        return tuple(out)
+
+    def attention(kv, plan, tasks):
+        peaks = None
+        for i in range(-1, len(plan)):
+            here = plan[i] if i >= 0 else []
+            there = plan[i + 1] if i + 1 < len(plan) else []
+            side = i % 2
+            rows, rows_next = [u[0] for u in here], [u[0] for u in there]
+            queries = [q_of[j, r].T for _, (q_of, j, r), _ in there]
+            tops = [jnp.max(p, axis=0, keepdims=True) for p in peaks] if here else []
+            for u in range(len(here)):
+                accs[u][...] = jnp.zeros((HEAD_DIM, TILE), jnp.float32)
+
+            def body(g, carry):
+                new_peaks = score(kv, rows_next, 1 - side, g, carry[0], queries)
+                return new_peaks, blend(kv, rows, side, g, carry[1], tops)
+
+            peaks, totals = lax.fori_loop(0, STEPS, body, ((lowest,) * len(there), (nothing,) * len(here)))
+            for u, (_, _, (dst, r)) in enumerate(here):
+                o = accs[u][...] * (1.0 / jnp.sum(totals[u], axis=0, keepdims=True))
+                dst[r, :] = o.T.astype(jnp.bfloat16)
+            if i in tasks:
+                tasks[i]()
+
+    def tile_rows(i):
+        return pl.ds(i * TILE, TILE)
+
+    def plan_of(j):
+        return [
+            [
+                (i, (q_own, j, i), (att.at[y, own_a + j], tile_rows(i))),
+                (ROW_TILES + i, (q_pair, j, i), (back.at[j], tile_rows(i))),
+            ]
+            for i in range(ROW_TILES)
+        ]
+
+    positions = [own_a, own_a + 1, pair_a, pair_a + 1, 4]
+
+    def y_send(n):
+        send(att.at[y, positions[n]], att.at[y, positions[n]], y_sem.at[0, n], to_y[0])
+        send(att.at[y, positions[n]], att.at[y, positions[n]], y_sem.at[1, n], to_y[2])
+
+    def y_parts(n):
+        cut = (3 if n % 2 == 0 else 2) * TILE
+        return pl.ds(0, cut), pl.ds(cut, ROWS - cut)
+
+    def y_pass(n):
+        first, second = y_parts(n)
+        arrived(att.at[y_left, positions[n]], y_sem.at[0, n], to_y[2])
+        part = att.at[y_left, positions[n], first]
+        send(part, part, y_far_sem.at[0, n], to_y[0])
+        arrived(att.at[y_right, positions[n]], y_sem.at[1, n], to_y[0])
+        part = att.at[y_right, positions[n], second]
+        send(part, part, y_far_sem.at[1, n], to_y[2])
+
+    def y_far(n):
+        first, second = y_parts(n)
+        arrived(att.at[y_opposite, positions[n], first], y_far_sem.at[0, n], to_y[2])
+        arrived(att.at[y_opposite, positions[n], second], y_far_sem.at[1, n], to_y[0])
+
+    def give_back(j):
+        send(back.at[j], att.at[y, own_a + j], ret_sem.at[j], to_pair)
+
+    def given_back(j):
+        arrived(att.at[y, pair_a + j], ret_sem.at[j], to_pair)
+        y_send(2 + j)
+
+    ours_columns = pl.ds(pl.multiple_of(zh * ROWS, TILE), ROWS)
+    theirs_columns = pl.ds(pl.multiple_of((1 - zh) * ROWS, TILE), ROWS)
+
+    def product(units, rows, columns):
+        lhs = jnp.concatenate([att[n, positions[u], rows, :] for u in units for n in range(RING)], axis=1)
+        rhs = jnp.concatenate([panel[n, head_columns(positions[u]), columns] for u in units for n in range(RING)], axis=0)
+        return jnp.dot(lhs, rhs, preferred_element_type=jnp.float32)
+
+    def contract(units, first):
+        def one(c, _):
+            rows = pl.ds(pl.multiple_of(c * TILE, TILE), TILE)
+            for total, columns in ((theirs, theirs_columns), (mine, ours_columns)):
+                p = product(units, rows, columns)
+                total[rows, :] = p if first else total[rows, :] + p
+            return 0
+
+        lax.fori_loop(0, ROW_TILES, one, 0)
+
+    def panel_here():
+        for d in range(3):
+            arrived(panel.at[lax.rem(y + 3 - d, RING), half], w_sem.at[d], to_y[2 - d])
+        local[3].wait()
+        for d in range(RING):
+            y_ = lax.rem(y + d, RING)
+            send(panel.at[y_, half], panel.at[y_, half], w_sib_sem.at[d], to_sib)
+
+    def after_a1():
+        ring_pass(B0, "b", kvb, zl)
+
+    def after_a3():
+        ring_pass(B1, "b", kvb, other)
+        ring_send(H0, kvh, zl, x)
+        to_sibling("h", kvh, zl, x)
+
+    attention(kva, plan_of(0), {1: after_a1, 3: after_a3})
+    give_back(0)
+    y_send(0)
+    arrived(block(kvh, other, x), z_sem.at[3], to_pair)
+    ring_send(V1, kvh, other, x, v_part)
+    to_sibling("h", kvh, other, x)
+    ring_far(B0, "b", kvb, zl)
+    ring_far(B1, "b", kvb, other)
+    panel_here()
+    from_sibling("b")
+
+    v_first, v_second = pl.ds(0, 3), pl.ds(3, 2)
+
+    def v_block(x_, rows=None):
+        at = kvh.at[seq_of(other, x_, core), 1]
+        return at if rows is None else at.at[rows]
+
+    def after_b1():
+        given_back(0)
+        ring_pass(H0, "h", kvh, zl)
+        for n, x_ in ((4, left), (5, right)):
+            send(block(kvh, zl, x_, k_part), block(kvh, zl, x_, k_part), z_sem.at[n], to_pair)
+        y_pass(0)
+
+    def after_b3():
+        arrived(block(kvh, other, left, v_part), x_sem.at[0, V1], to_left)
+        send(v_block(left, v_first), v_block(left, v_first), far_sem.at[0, V1], to_right)
+        arrived(block(kvh, other, right, v_part), x_sem.at[1, V1], to_right)
+        send(v_block(right, v_second), v_block(right, v_second), far_sem.at[1, V1], to_left)
+        to_sibling("h", kvh, other, left, v_part)
+        to_sibling("h", kvh, other, right, v_part)
+        y_pass(2)
+
+    attention(kvb, plan_of(1), {1: after_b1, 3: after_b3})
+    give_back(1)
+    y_send(1)
+    ring_far(H0, "h", kvh, zl)
+    send(block(kvh, zl, opposite, k_part), block(kvh, zl, opposite, k_part), z_sem.at[6], to_pair)
+    arrived(v_block(opposite, v_first), far_sem.at[0, V1], to_left)
+    arrived(v_block(opposite, v_second), far_sem.at[1, V1], to_right)
+    to_sibling("h", kvh, other, opposite, v_part)
+    for n, x_ in ((4, left), (5, right)):
+        arrived(block(kvh, other, x_, k_part), z_sem.at[n], to_pair)
+        to_sibling("h", kvh, other, x_, k_part)
+    given_back(1)
+    y_far(0)
+    y_far(2)
+    for d in range(RING):
+        arrived(panel.at[lax.rem(y + d, RING), other_half], w_sib_sem.at[d], to_sib)
+    contract((0, 2), True)
+    arrived(block(kvh, other, opposite, k_part), z_sem.at[6], to_pair)
+    to_sibling("h", kvh, other, opposite, k_part)
+    y_pass(1)
+    from_sibling("h")
+
+    units = [
+        (i, (q_own, 2, i), (att.at[y, 4], tile_rows(i))) for i in range(ROW_TILES)
+    ]
+    attention(kvh, [units[0:2], units[2:4], units[4:5]], {0: lambda: y_pass(3)})
+    y_send(4)
+    y_far(1)
+    y_far(3)
+    contract((1, 3), False)
+    y_pass(4)
+    y_far(4)
+    for c in range(ROW_TILES):
+        rows = tile_rows(c)
+        sent[rows, :] = (theirs[rows, :] + product((4,), rows, theirs_columns)).astype(sent.dtype)
+        send(sent.at[rows], got.at[rows], sum_sem.at[c], to_sum)
+    local[4].wait()
+    for c in range(ROW_TILES):
+        rows = tile_rows(c)
+        mine[rows, :] = mine[rows, :] + product((4,), rows, ours_columns)
+    for c in range(ROW_TILES):
+        rows = tile_rows(c)
+        arrived(got.at[rows], sum_sem.at[c], to_sum)
+        projected = mine[rows, :] + got[rows, :].astype(jnp.float32)
+        out = res_ref[rows, :].astype(jnp.float32) + gate_ref[...] * (projected + bias_ref[...])
+        out_ref[rows, :] = out.astype(out_ref.dtype)
+    for c in sends:
+        c.wait_send()
+
+
+def whole(owners, starts, bars, q, k, v, w, bias, gate, residual):
+    bf16, f32 = jnp.bfloat16, jnp.float32
+
+    def by_tile(array):
+        return array.reshape(ROW_TILES, TILE, ROWS)
+
+    smem, vmem, anywhere = (
+        pl.BlockSpec(memory_space=pltpu.SMEM),
+        pl.BlockSpec(memory_space=pltpu.VMEM),
+        pl.BlockSpec(memory_space=pl.ANY),
+    )
+    dma = pltpu.SemaphoreType.DMA
+    return pl.pallas_call(
+        whole_kernel,
+        out_shape=jax.ShapeDtypeStruct((ROWS, ROWS), bf16),
+        in_specs=[smem, smem, smem, anywhere, anywhere, anywhere, anywhere, vmem, vmem, anywhere],
+        out_specs=vmem,
+        scratch_shapes=[
+            pltpu.VMEM((12, ROW_TILES, TILE, HEAD_DIM), bf16),
+            pltpu.VMEM((5, ROW_TILES, TILE, HEAD_DIM), bf16),
+            pltpu.VMEM((SEQ, 2, ROW_TILES, TILE, HEAD_DIM), bf16),
+            pltpu.VMEM((SEQ, 2, ROW_TILES, TILE, HEAD_DIM), bf16),
+            pltpu.VMEM((SEQ, 2, ROW_TILES, TILE, HEAD_DIM), bf16),
+            pltpu.VMEM((3, ROW_TILES, TILE, HEAD_DIM), bf16),
+            pltpu.VMEM((2, ROW_TILES, TILE, HEAD_DIM), bf16),
+            pltpu.VMEM((RING, 5, ROWS, HEAD_DIM), bf16),
+            pltpu.VMEM((2, ROWS, HEAD_DIM), bf16),
+            pltpu.VMEM((RING, ROWS, 2 * ROWS), bf16),
+            pltpu.VMEM((ROWS, ROWS), f32),
+            pltpu.VMEM((ROWS, ROWS), f32),
+            pltpu.VMEM((ROWS, ROWS), bf16),
+            pltpu.VMEM((ROWS, ROWS), bf16),
+            pltpu.VMEM((ROWS, ROWS), bf16),
+        ]
+        + [pltpu.VMEM((LIMIT, TILE, TILE), f32)] * 4
+        + [pltpu.VMEM((HEAD_DIM, TILE), f32)] * 2
+        + [
+            dma((12,)), dma((8,)), dma((96,)), dma((7,)), dma((2, 6)), dma((2, 6)), dma((28,)), dma((3,)), dma((4,)),
+            dma((2,)), dma((2, 5)), dma((2, 5)), dma((5,)),
+        ],
+        compiler_params=pltpu.CompilerParams(collective_id=2, has_side_effects=True, vmem_limit_bytes=62 << 20),
+        name="whole",
+    )(owners, starts, bars, by_tile(q), by_tile(k), by_tile(v), w, bias, gate, residual)
 
 
 def tile_lists(tile_mask):
@@ -506,16 +971,27 @@
     allowed = rows > 0
     at = jnp.arange(TILE_COUNT, dtype=jnp.int32)
     before = jnp.sum(jnp.where(allowed[:, None, :] & (at[None, None, :] < at[None, :, None]), 1, 0), axis=2)
-    hit = allowed[:, None, :] & (before[:, None, :] == at[None, :, None])
+    hit = allowed[:, None, :] & (before[:, None, :] == at[None, :LIMIT, None])
     tiles = jnp.sum(jnp.where(hit, at[None, None, :], 0), axis=2)
-    return tiles.astype(jnp.int32), jnp.sum(allowed, axis=1).astype(jnp.int32)
+    tiles = tiles.astype(jnp.int32)
+    bars = jnp.where(at[None, :LIMIT] < jnp.sum(allowed, axis=1)[:, None], 0.0, MASKED).astype(jnp.float32)
+    return tiles // ROW_TILES, tiles % ROW_TILES, bars
 
 
 def local(queries, key_states, value_states, tile_mask, out_weight, out_bias, residual, gate_scale):
-    tiles, counts = tile_lists(tile_mask)
-    kv, q, panel = gather(queries, key_states, value_states, out_weight)
-    o = attend(tiles, counts, q, kv)
-    return project(o, panel.reshape(RING * ROWS, 2 * ROWS), out_bias[None, :], gate_scale[None, :], residual)
+    bias, gate = out_bias[None, :], gate_scale[None, :]
+
+    def by_lists(_):
+        owners, starts, bars = tile_lists(tile_mask)
+        return whole(owners, starts, bars, queries, key_states, value_states, out_weight, bias, gate, residual)
+
+    def in_parts(_):
+        kv, q, panel = gather(queries, key_states, value_states, out_weight)
+        o = attend(tile_mask, q, kv)
+        return project(o, panel.reshape(RING * ROWS, 2 * ROWS), bias, gate, residual)
+
+    longest = jnp.max(jnp.sum((tile_mask > 0).astype(jnp.int32), axis=1))
+    return lax.cond(longest <= LIMIT, by_lists, in_parts, 0)
 
 
 def solution(mesh):

time: 152 us -> 126 us (0.83)
  the two profiles are of different devices: /device:TPU:4 before, /device:TPU:0 now
where the time goes in v3:
time: 126 us; the launch traced here: 124 us
  Pallas kernels  117 us (93%)
  other arithmetic  3.51 us (3%)
  local copies, waits for them, and re-layouts  2.99 us (2%)
    pallas_call x1, Pallas kernels, whole(): pl.pallas_call(whole_kernel, out_shape=jax.ShapeDtypeStruct((ROWS, ROWS),...  117 us

profile of v3, /device:TPU:0, one launch (start us, length us, event | category | flops | bytes accessed | tf_op | source)
XLA Modules:
  0.0 124.4 jit_solution(10831812308456274209)
XLA Ops:
  0.0 0.9 convert_reduce_fusion.1
  0.9 0.6 reduce_max.9
  2.2 0.7 broadcast_in_dim.43
  2.9 0.7 broadcast_in_dim.44
  3.6 120.0 %conditional.1 = (bf16[640,640]{1,0:T(8,128)(2,1)S(1)}) conditional(s32[]{:T(128)} %convert_element_type.10, (bf16[640,640]{1,0:T(8,128)(2,1)}, bf16[640,640]{1,0:T(8,128)(2,1)}, bf16[640,640]{1,0:T(8,128)(2,1)}, bf16[640,5120]{1,0:T(8,128)(2,1)}, s32[80,80]{1,0:T(8,128)}, /*index=5*/f32[1,640]{1,0:T(1,128)S(1)}, f32[1,640]{1,0:T(1,128)S(1)}, ...), branch_computations={%region_2.0_spmd, %region_3.7_spmd} | conditional | flops 334028 | bytes 3379264 | solution.py:994
  3.6 0.7 constant_dynamic-slice_fusion.1
  4.3 0.1 convert_reduce_fusion
  4.4 0.7 compare_select_fusion.bars_ref
  5.1 0.3 select_reduce_fusion
  5.3 0.3 select_reduce_fusion.1
  5.7 0.6 add_select_fusion
  6.3 117.2 %whole.1 = bf16[640,640]{1,0:T(8,128)(2,1)S(1)} custom-call(s32[10,40]{1,0:T(8,128)} %get-tuple-element.65.owners_ref, s32[10,40]{1,0:T(8,128)} %get-tuple-element.64.starts_ref, f32[10,40]{1,0:T(8,128)} %compare_select_fusion.bars_ref, bf16[5,128,640]{2,1,0:T(8,128)(2,1)} %bitcast.6, bf16[5,128,640]{2,1,0:T(8,128)(2,1)} %bitcast.7, ...), custom_call_target="tpu_custom_call" | custom-call | tf_op jit(solution)/shard_map/cond/branch_1_fun/whole/pallas_call | solution.py:931
  123.5 0.9 copy.14
  (2 shorter events, 0.0 us)

commit v4 on v3

--- a/solution.py
+++ b/solution.py
@@ -599,22 +599,23 @@
     ]
     for c in local:
         c.start()
-    for c in stage_copies:
+
+    def turn(piece):
+        def one(r, _):
+            stage[2 * piece + 1, r] = raw_values[piece, r].T
+            return 0
+
+        lax.fori_loop(0, ROW_TILES, one, 0)
+
+    for c in stage_copies[:4]:
         c.wait()
-
-    def turn(n, _):
-        piece = lax.div(n, ROW_TILES)
-        r = n - piece * ROW_TILES
-        stage[2 * piece + 1, r] = raw_values[piece, r].T
-        return 0
-
-    lax.fori_loop(0, 5 * ROW_TILES, turn, 0)
+    turn(0)
+    turn(3)
     own = [
         pltpu.make_async_copy(stage.at[pl.ds(2 * n, 2)], kv.at[me], local_sem.at[5 + n])
         for n, kv in enumerate((kva, kvb, kvh))
     ]
-    for c in own:
-        c.start()
+    own[0].start()
     pl.semaphore_wait(barrier, len(neighbours))
 
     sends = []
@@ -668,13 +669,22 @@
 
     A0, A1, B0, B1, H0, V1 = range(6)
     send(stage.at[pl.ds(6, 2)], kva.at[me], z_sem.at[0], to_pair)
-    own[0].wait()
-    ring_send(A0, kva, zl, x)
-    to_sibling("a", kva, zl, x)
+    send(stage.at[pl.ds(0, 2)], kva.at[me], x_sem.at[0, A0], to_right)
+    send(stage.at[pl.ds(0, 2)], kva.at[me], x_sem.at[1, A0], to_left)
+    send(stage.at[pl.ds(0, 2)], kva.at[me], sib_sem.at[0], to_sib)
+    sib_count[0] = 1
+    sib_waits["a"].append((0, kva, zl, x, both_parts))
     for d in range(3):
         send(w_ref.at[half, columns_of(lax.rem(y + d + 1, RING))], panel.at[y, half], w_sem.at[d], to_y[d])
-    own[1].wait()
-    own[2].wait()
+    for c in stage_copies[4:]:
+        c.wait()
+    turn(1)
+    turn(4)
+    turn(2)
+    for c in own[1:]:
+        c.start()
+    for c in own:
+        c.wait()
     arrived(block(kva, other, x), z_sem.at[0], to_pair)
     ring_send(A1, kva, other, x)
     send(stage.at[pl.ds(8, 2)], kvb.at[me], z_sem.at[1], to_pair)
@@ -770,34 +780,40 @@
 
     positions = [own_a, own_a + 1, pair_a, pair_a + 1, 4]
 
-    def y_send(n):
-        send(att.at[y, positions[n]], att.at[y, positions[n]], y_sem.at[0, n], to_y[0])
-        send(att.at[y, positions[n]], att.at[y, positions[n]], y_sem.at[1, n], to_y[2])
-
-    def y_parts(n):
-        cut = (3 if n % 2 == 0 else 2) * TILE
-        return pl.ds(0, cut), pl.ds(cut, ROWS - cut)
-
-    def y_pass(n):
-        first, second = y_parts(n)
-        arrived(att.at[y_left, positions[n]], y_sem.at[0, n], to_y[2])
-        part = att.at[y_left, positions[n], first]
-        send(part, part, y_far_sem.at[0, n], to_y[0])
-        arrived(att.at[y_right, positions[n]], y_sem.at[1, n], to_y[0])
-        part = att.at[y_right, positions[n], second]
-        send(part, part, y_far_sem.at[1, n], to_y[2])
-
-    def y_far(n):
-        first, second = y_parts(n)
-        arrived(att.at[y_opposite, positions[n], first], y_far_sem.at[0, n], to_y[2])
-        arrived(att.at[y_opposite, positions[n], second], y_far_sem.at[1, n], to_y[0])
-
-    def give_back(j):
-        send(back.at[j], att.at[y, own_a + j], ret_sem.at[j], to_pair)
-
-    def given_back(j):
-        arrived(att.at[y, pair_a + j], ret_sem.at[j], to_pair)
-        y_send(2 + j)
+    row_groups = {0: [(0, 640)], 1: [(0, 384), (384, 256)], 2: [(0, 640)], 3: [(0, 384), (384, 256)]}
+    row_groups[4] = [(0, 256), (256, 256), (512, 128)]
+    first_sem = {0: 0, 1: 1, 2: 3, 3: 4, 4: 6}
+
+    def y_block(n, y_, start, count):
+        return att.at[y_, positions[n], pl.ds(start, count)]
+
+    def y_send(n, g=0):
+        part = y_block(n, y, *row_groups[n][g])
+        send(part, part, y_sem.at[0, first_sem[n] + g], to_y[0])
+        send(part, part, y_sem.at[1, first_sem[n] + g], to_y[2])
+
+    def y_pass(n, g=0):
+        start, count = row_groups[n][g]
+        arrived(y_block(n, y_left, start, count), y_sem.at[0, first_sem[n] + g], to_y[2])
+        part = y_block(n, y_left, start, count // 2)
+        send(part, part, y_far_sem.at[0, first_sem[n] + g], to_y[0])
+        arrived(y_block(n, y_right, start, count), y_sem.at[1, first_sem[n] + g], to_y[0])
+        part = y_block(n, y_right, start + count // 2, count // 2)
+        send(part, part, y_far_sem.at[1, first_sem[n] + g], to_y[2])
+
+    def y_far(n, g=0):
+        start, count = row_groups[n][g]
+        arrived(y_block(n, y_opposite, start, count // 2), y_far_sem.at[0, first_sem[n] + g], to_y[2])
+        arrived(y_block(n, y_opposite, start + count // 2, count // 2), y_far_sem.at[1, first_sem[n] + g], to_y[0])
+
+    def give_back(j, g=0):
+        rows = pl.ds(*row_groups[2 + j][g])
+        send(back.at[j, rows], att.at[y, own_a + j, rows], ret_sem.at[j + g], to_pair)
+
+    def given_back(j, g=0):
+        rows = pl.ds(*row_groups[2 + j][g])
+        arrived(att.at[y, pair_a + j, rows], ret_sem.at[j + g], to_pair)
+        y_send(2 + j, g)
 
     ours_columns = pl.ds(pl.multiple_of(zh * ROWS, TILE), ROWS)
     theirs_columns = pl.ds(pl.multiple_of((1 - zh) * ROWS, TILE), ROWS)
@@ -807,10 +823,10 @@
         rhs = jnp.concatenate([panel[n, head_columns(positions[u]), columns] for u in units for n in range(RING)], axis=0)
         return jnp.dot(lhs, rhs, preferred_element_type=jnp.float32)
 
-    def contract(units, first):
+    def contract(units, first, parts):
         def one(c, _):
             rows = pl.ds(pl.multiple_of(c * TILE, TILE), TILE)
-            for total, columns in ((theirs, theirs_columns), (mine, ours_columns)):
+            for total, columns in parts:
                 p = product(units, rows, columns)
                 total[rows, :] = p if first else total[rows, :] + p
             return 0
@@ -866,9 +882,13 @@
         to_sibling("h", kvh, other, right, v_part)
         y_pass(2)
 
-    attention(kvb, plan_of(1), {1: after_b1, 3: after_b3})
-    give_back(1)
-    y_send(1)
+    def after_b2():
+        give_back(1, 0)
+        y_send(1, 0)
+
+    attention(kvb, plan_of(1), {1: after_b1, 2: after_b2, 3: after_b3})
+    give_back(1, 1)
+    y_send(1, 1)
     ring_far(H0, "h", kvh, zl)
     send(block(kvh, zl, opposite, k_part), block(kvh, zl, opposite, k_part), z_sem.at[6], to_pair)
     arrived(v_block(opposite, v_first), far_sem.at[0, V1], to_left)
@@ -877,40 +897,52 @@
     for n, x_ in ((4, left), (5, right)):
         arrived(block(kvh, other, x_, k_part), z_sem.at[n], to_pair)
         to_sibling("h", kvh, other, x_, k_part)
-    given_back(1)
+    given_back(1, 0)
+    y_pass(1, 0)
     y_far(0)
     y_far(2)
     for d in range(RING):
         arrived(panel.at[lax.rem(y + d, RING), other_half], w_sib_sem.at[d], to_sib)
-    contract((0, 2), True)
+    contract((0, 2), True, ((theirs, theirs_columns), (mine, ours_columns)))
+    given_back(1, 1)
     arrived(block(kvh, other, opposite, k_part), z_sem.at[6], to_pair)
     to_sibling("h", kvh, other, opposite, k_part)
-    y_pass(1)
+    y_pass(1, 1)
+    y_pass(3, 0)
     from_sibling("h")
 
     units = [
         (i, (q_own, 2, i), (att.at[y, 4], tile_rows(i))) for i in range(ROW_TILES)
     ]
-    attention(kvh, [units[0:2], units[2:4], units[4:5]], {0: lambda: y_pass(3)})
-    y_send(4)
-    y_far(1)
-    y_far(3)
-    contract((1, 3), False)
-    y_pass(4)
-    y_far(4)
-    for c in range(ROW_TILES):
-        rows = tile_rows(c)
-        sent[rows, :] = (theirs[rows, :] + product((4,), rows, theirs_columns)).astype(sent.dtype)
-        send(sent.at[rows], got.at[rows], sum_sem.at[c], to_sum)
+
+    def after_h0():
+        y_send(4, 0)
+        y_pass(3, 1)
+
+    def after_h1():
+        y_send(4, 1)
+        y_pass(4, 0)
+
+    attention(kvh, [units[0:2], units[2:4], units[4:5]], {0: after_h0, 1: after_h1, 2: lambda: y_send(4, 2)})
+    y_pass(4, 1)
+    for n in (1, 3):
+        for g in range(2):
+            y_far(n, g)
+    for g, tiles in enumerate(((0, 1), (2, 3), (4,))):
+        y_far(4, g)
+        for c in tiles:
+            rows = tile_rows(c)
+            sent[rows, :] = (theirs[rows, :] + product((1, 3, 4), rows, theirs_columns)).astype(sent.dtype)
+            send(sent.at[rows], got.at[rows], sum_sem.at[c], to_sum)
+        if g == 0:
+            y_pass(4, 2)
     local[4].wait()
-    for c in range(ROW_TILES):
-        rows = tile_rows(c)
-        mine[rows, :] = mine[rows, :] + product((4,), rows, ours_columns)
+    contract((1, 3, 4), False, ((mine, ours_columns),))
     for c in range(ROW_TILES):
         rows = tile_rows(c)
         arrived(got.at[rows], sum_sem.at[c], to_sum)
         projected = mine[rows, :] + got[rows, :].astype(jnp.float32)
-        out = res_ref[rows, :].astype(jnp.float32) + gate_ref[...] * (projected + bias_ref[...])
+        out = res_ref[rows, :].astype(jnp.float32) + gate_ref[...][None, :] * (projected + bias_ref[...][None, :])
         out_ref[rows, :] = out.astype(out_ref.dtype)
     for c in sends:
         c.wait_send()
@@ -953,8 +985,8 @@
         + [pltpu.VMEM((LIMIT, TILE, TILE), f32)] * 4
         + [pltpu.VMEM((HEAD_DIM, TILE), f32)] * 2
         + [
-            dma((12,)), dma((8,)), dma((96,)), dma((7,)), dma((2, 6)), dma((2, 6)), dma((28,)), dma((3,)), dma((4,)),
-            dma((2,)), dma((2, 5)), dma((2, 5)), dma((5,)),
+            dma((12,)), dma((8,)), dma((128,)), dma((7,)), dma((2, 6)), dma((2, 6)), dma((28,)), dma((3,)), dma((4,)),
+            dma((3,)), dma((2, 9)), dma((2, 9)), dma((5,)),
         ],
         compiler_params=pltpu.CompilerParams(collective_id=2, has_side_effects=True, vmem_limit_bytes=62 << 20),
         name="whole",
@@ -979,7 +1011,7 @@
 
 
 def local(queries, key_states, value_states, tile_mask, out_weight, out_bias, residual, gate_scale):
-    bias, gate = out_bias[None, :], gate_scale[None, :]
+    bias, gate = out_bias, gate_scale
 
     def by_lists(_):
         owners, starts, bars = tile_lists(tile_mask)
@@ -988,7 +1020,7 @@
     def in_parts(_):
         kv, q, panel = gather(queries, key_states, value_states, out_weight)
         o = attend(tile_mask, q, kv)
-        return project(o, panel.reshape(RING * ROWS, 2 * ROWS), bias, gate, residual)
+        return project(o, panel.reshape(RING * ROWS, 2 * ROWS), bias[None, :], gate[None, :], residual)
 
     longest = jnp.max(jnp.sum((tile_mask > 0).astype(jnp.int32), axis=1))
     return lax.cond(longest <= LIMIT, by_lists, in_parts, 0)

time: 126 us -> 118 us (0.937); the launches traced: 124 us -> 118 us
  Pallas kernels: 117 us -> 112 us
  local copies, waits for them, and re-layouts: 2.99 us -> 1.63 us
    pallas_call x1, Pallas kernels: 117 us -> 112 us  [whole(): pl.pallas_call(whole_kernel, out_shape=jax.ShapeDtypeStruct((ROWS, ROWS),...]
    broadcast_in_dim x2 -> x0, local copies, waits for them, and re-layouts: 1.38 us -> none  [local(): bias, gate = (out_bias[None, :], gate_scale[None, :])]
where the time goes in v4:
time: 118 us
  Pallas kernels  112 us (95%)
  other arithmetic  3.5 us (3%)
  local copies, waits for them, and re-layouts  1.63 us (1%)
    pallas_call x1, Pallas kernels, whole(): pl.pallas_call(whole_kernel, out_shape=jax.ShapeDtypeStruct((ROWS, ROWS),...  112 us

profile of v4, /device:TPU:0, one launch (start us, length us, event | category | flops | bytes accessed | tf_op | source)
XLA Modules:
  0.0 118.1 jit_solution(12892130249943168808)
XLA Ops:
  0.0 0.9 convert_reduce_fusion.1
  0.9 0.6 reduce_max.9
  2.2 115.0 %conditional.1 = (bf16[640,640]{1,0:T(8,128)(2,1)S(1)}) conditional(s32[]{:T(128)} %convert_element_type.10, (bf16[640,640]{1,0:T(8,128)(2,1)}, bf16[640,640]{1,0:T(8,128)(2,1)}, bf16[640,640]{1,0:T(8,128)(2,1)}, bf16[640,5120]{1,0:T(8,128)(2,1)}, s32[80,80]{1,0:T(8,128)}, /*index=5*/f32[640]{0:T(1024)}, f32[640]{0:T(1024)}, ...), branch_computations={%region_2.0_spmd, %region_3.7_spmd} | conditional | flops 334028 | bytes 3410040 | solution.py:1026
  2.5 0.7 constant_dynamic-slice_fusion.1
  3.2 0.1 convert_reduce_fusion
  3.3 0.3 select_reduce_fusion
  3.6 0.3 select_reduce_fusion.1
  3.9 0.6 add_select_fusion
  4.5 0.7 compare_select_fusion.bars_ref
  5.2 112.0 %whole.1 = bf16[640,640]{1,0:T(8,128)(2,1)S(1)} custom-call(s32[10,40]{1,0:T(8,128)} %get-tuple-element.65.owners_ref, s32[10,40]{1,0:T(8,128)} %get-tuple-element.64.starts_ref, f32[10,40]{1,0:T(8,128)} %compare_select_fusion.bars_ref, bf16[5,128,640]{2,1,0:T(8,128)(2,1)} %bitcast.6, bf16[5,128,640]{2,1,0:T(8,128)(2,1)} %bitcast.7, ...), custom_call_target="tpu_custom_call" | custom-call | tf_op jit(solution)/shard_map/cond/branch_1_fun/whole/pallas_call | solution.py:963
  117.2 0.9 copy.14
  (2 shorter events, 0.0 us)

commit v5 on v4

--- a/solution.py
+++ b/solution.py
@@ -1,3 +1,5 @@
+import functools
+
 import jax
 import jax.numpy as jnp
 from jax import lax
@@ -527,7 +529,6 @@
 
 
 LIMIT = 40
-STEPS = LIMIT // GROUP
 KEYS_OF = pl.ds(0, 1)
 VALUES_OF = pl.ds(1, 1)
 
@@ -712,38 +713,38 @@
     nothing = jnp.zeros((8, TILE), jnp.float32)
 
     def place_of(row, n):
-        return owners_ref[row, n], starts_ref[row, n]
-
-    def score(kv, rows, side, g, peaks, queries):
+        return owners_ref[n, row], starts_ref[n, row]
+
+    def score(kv, rows, side, g, peaks, queries, group):
         out = []
         for u, row in enumerate(rows):
-            at = [place_of(row, g * GROUP + t) for t in range(GROUP)]
+            at = [place_of(row, g * group + t) for t in range(group)]
             keys = jnp.concatenate([kv[o, 0, r] for o, r in at], axis=0)
             s = jnp.dot(keys, queries[u], preferred_element_type=jnp.float32)
             top = peaks[u]
-            for t in range(GROUP):
-                part = s[t * TILE : (t + 1) * TILE] + bars_ref[row, g * GROUP + t]
-                scores[side][u][g * GROUP + t] = part
+            for t in range(group):
+                part = s[t * TILE : (t + 1) * TILE] + bars_ref[g * group + t, row]
+                scores[side][u][g * group + t] = part
                 top = jnp.maximum(top, jnp.max(part.reshape(TILE // 8, 8, TILE), axis=0))
             out.append(top)
         return tuple(out)
 
-    def blend(kv, rows, side, g, totals, peaks):
+    def blend(kv, rows, side, g, totals, peaks, group):
         out = []
         for u, row in enumerate(rows):
             total = totals[u]
             weights = []
-            for t in range(GROUP):
-                w = jnp.exp2((scores[side][u][g * GROUP + t] - peaks[u]) * factor)
+            for t in range(group):
+                w = jnp.exp2((scores[side][u][g * group + t] - peaks[u]) * factor)
                 total = total + jnp.sum(w.reshape(TILE // 8, 8, TILE), axis=0)
                 weights.append(w.astype(jnp.bfloat16))
-            at = [place_of(row, g * GROUP + t) for t in range(GROUP)]
+            at = [place_of(row, g * group + t) for t in range(group)]
             values = jnp.concatenate([kv[o, 1, r] for o, r in at], axis=1)
             accs[u][...] += jnp.dot(values, jnp.concatenate(weights, axis=0), preferred_element_type=jnp.float32)
             out.append(total)
         return tuple(out)
 
-    def attention(kv, plan, tasks):
+    def attention(kv, plan, tasks, group=GROUP):
         peaks = None
         for i in range(-1, len(plan)):
             here = plan[i] if i >= 0 else []
@@ -756,10 +757,10 @@
                 accs[u][...] = jnp.zeros((HEAD_DIM, TILE), jnp.float32)
 
             def body(g, carry):
-                new_peaks = score(kv, rows_next, 1 - side, g, carry[0], queries)
-                return new_peaks, blend(kv, rows, side, g, carry[1], tops)
-
-            peaks, totals = lax.fori_loop(0, STEPS, body, ((lowest,) * len(there), (nothing,) * len(here)))
+                new_peaks = score(kv, rows_next, 1 - side, g, carry[0], queries, group)
+                return new_peaks, blend(kv, rows, side, g, carry[1], tops, group)
+
+            peaks, totals = lax.fori_loop(0, LIMIT // group, body, ((lowest,) * len(there), (nothing,) * len(here)))
             for u, (_, _, (dst, r)) in enumerate(here):
                 o = accs[u][...] * (1.0 / jnp.sum(totals[u], axis=0, keepdims=True))
                 dst[r, :] = o.T.astype(jnp.bfloat16)
@@ -781,7 +782,7 @@
     positions = [own_a, own_a + 1, pair_a, pair_a + 1, 4]
 
     row_groups = {0: [(0, 640)], 1: [(0, 384), (384, 256)], 2: [(0, 640)], 3: [(0, 384), (384, 256)]}
-    row_groups[4] = [(0, 256), (256, 256), (512, 128)]
+    row_groups[4] = [(TILE * i, TILE) for i in range(ROW_TILES)]
     first_sem = {0: 0, 1: 1, 2: 3, 3: 4, 4: 6}
 
     def y_block(n, y_, start, count):
@@ -915,27 +916,29 @@
         (i, (q_own, 2, i), (att.at[y, 4], tile_rows(i))) for i in range(ROW_TILES)
     ]
 
-    def after_h0():
-        y_send(4, 0)
-        y_pass(3, 1)
-
-    def after_h1():
-        y_send(4, 1)
-        y_pass(4, 0)
-
-    attention(kvh, [units[0:2], units[2:4], units[4:5]], {0: after_h0, 1: after_h1, 2: lambda: y_send(4, 2)})
-    y_pass(4, 1)
-    for n in (1, 3):
-        for g in range(2):
-            y_far(n, g)
-    for g, tiles in enumerate(((0, 1), (2, 3), (4,))):
-        y_far(4, g)
-        for c in tiles:
-            rows = tile_rows(c)
-            sent[rows, :] = (theirs[rows, :] + product((1, 3, 4), rows, theirs_columns)).astype(sent.dtype)
-            send(sent.at[rows], got.at[rows], sum_sem.at[c], to_sum)
-        if g == 0:
-            y_pass(4, 2)
+    def sum_out(c):
+        y_far(4, c)
+        rows = tile_rows(c)
+        sent[rows, :] = (theirs[rows, :] + product((1, 3, 4), rows, theirs_columns)).astype(sent.dtype)
+        send(sent.at[rows], got.at[rows], sum_sem.at[c], to_sum)
+
+    def after_h(i):
+        y_send(4, i)
+        if i == 0:
+            y_pass(3, 1)
+        else:
+            y_pass(4, i - 1)
+        if i == 2:
+            for n in (1, 3):
+                for g in range(2):
+                    y_far(n, g)
+        if i >= 2:
+            sum_out(i - 2)
+
+    attention(kvh, [[u] for u in units], {i: functools.partial(after_h, i) for i in range(ROW_TILES)}, 2 * GROUP)
+    y_pass(4, 4)
+    sum_out(3)
+    sum_out(4)
     local[4].wait()
     contract((1, 3, 4), False, ((mine, ours_columns),))
     for c in range(ROW_TILES):
@@ -986,35 +989,67 @@
         + [pltpu.VMEM((HEAD_DIM, TILE), f32)] * 2
         + [
             dma((12,)), dma((8,)), dma((128,)), dma((7,)), dma((2, 6)), dma((2, 6)), dma((28,)), dma((3,)), dma((4,)),
-            dma((3,)), dma((2, 9)), dma((2, 9)), dma((5,)),
+            dma((3,)), dma((2, 11)), dma((2, 11)), dma((5,)),
         ],
         compiler_params=pltpu.CompilerParams(collective_id=2, has_side_effects=True, vmem_limit_bytes=62 << 20),
         name="whole",
     )(owners, starts, bars, by_tile(q), by_tile(k), by_tile(v), w, bias, gate, residual)
 
 
+def list_kernel(mask_ref, owners_ref, starts_ref, bars_ref, longest_ref):
+    zl, x, core, _, _ = place()
+    rows = []
+    for plane in (zl, 1 - zl):
+        first = ((plane * RING + x) * 2 + core) * ROW_TILES
+        rows += [mask_ref[pl.ds(first + i, 1), :] for i in range(ROW_TILES)]
+    allowed = jnp.where(jnp.concatenate(rows, axis=0) > 0, 1.0, 0.0)
+    square = (TILE_COUNT, TILE_COUNT)
+    earlier = lax.broadcasted_iota(jnp.int32, square, 0) < lax.broadcasted_iota(jnp.int32, square, 1)
+    before = jnp.dot(allowed, jnp.where(earlier, 1.0, 0.0), preferred_element_type=jnp.float32).astype(jnp.int32)
+    entry = lax.broadcasted_iota(jnp.int32, (LIMIT, TILE_COUNT), 0)
+    tile = lax.broadcasted_iota(jnp.int32, (LIMIT, TILE_COUNT), 1)
+    lane = lax.broadcasted_iota(jnp.int32, (LIMIT, 128), 1)
+    entry_column = lax.broadcasted_iota(jnp.int32, (LIMIT, 128), 0)
+    owner = jnp.zeros((LIMIT, TILE_COUNT), jnp.int32)
+    for n in range(1, SEQ):
+        owner = owner + jnp.where(tile >= n * ROW_TILES, 1, 0)
+    start = tile - owner * ROW_TILES
+    owners = jnp.zeros((LIMIT, 128), jnp.int32)
+    starts = jnp.zeros((LIMIT, 128), jnp.int32)
+    bars = jnp.full((LIMIT, 128), MASKED, jnp.float32)
+    for i in range(2 * ROW_TILES):
+        hit = (before[i : i + 1] == entry) & (allowed[i : i + 1] > 0.5)
+        count = jnp.sum(allowed[i : i + 1], axis=1, keepdims=True).astype(jnp.int32)
+        owners = jnp.where(lane == i, jnp.sum(jnp.where(hit, owner, 0), axis=1, keepdims=True), owners)
+        starts = jnp.where(lane == i, jnp.sum(jnp.where(hit, start, 0), axis=1, keepdims=True), starts)
+        bars = jnp.where((lane == i) & (entry_column < count), 0.0, bars)
+    owners_ref[...] = owners
+    starts_ref[...] = starts
+    bars_ref[...] = bars
+    longest_ref[0] = jnp.max(jnp.sum(jnp.where(mask_ref[...] > 0, 1, 0), axis=1, keepdims=True))
+
+
 def tile_lists(tile_mask):
-    zl, x, core, _, _ = place()
-    own = (zl * RING + x) * 2 + core
-    pair = ((1 - zl) * RING + x) * 2 + core
-    rows = jnp.concatenate(
-        [lax.dynamic_slice_in_dim(tile_mask, first * ROW_TILES, ROW_TILES, 0) for first in (own, pair)], axis=0
-    )
-    allowed = rows > 0
-    at = jnp.arange(TILE_COUNT, dtype=jnp.int32)
-    before = jnp.sum(jnp.where(allowed[:, None, :] & (at[None, None, :] < at[None, :, None]), 1, 0), axis=2)
-    hit = allowed[:, None, :] & (before[:, None, :] == at[None, :LIMIT, None])
-    tiles = jnp.sum(jnp.where(hit, at[None, None, :], 0), axis=2)
-    tiles = tiles.astype(jnp.int32)
-    bars = jnp.where(at[None, :LIMIT] < jnp.sum(allowed, axis=1)[:, None], 0.0, MASKED).astype(jnp.float32)
-    return tiles // ROW_TILES, tiles % ROW_TILES, bars
+    vmem, smem = pl.BlockSpec(memory_space=pltpu.VMEM), pl.BlockSpec(memory_space=pltpu.SMEM)
+    return pl.pallas_call(
+        list_kernel,
+        out_shape=[
+            jax.ShapeDtypeStruct((LIMIT, 128), jnp.int32),
+            jax.ShapeDtypeStruct((LIMIT, 128), jnp.int32),
+            jax.ShapeDtypeStruct((LIMIT, 128), jnp.float32),
+            jax.ShapeDtypeStruct((1,), jnp.int32),
+        ],
+        in_specs=[vmem],
+        out_specs=[vmem, vmem, vmem, smem],
+        name="tile_lists",
+    )(tile_mask)
 
 
 def local(queries, key_states, value_states, tile_mask, out_weight, out_bias, residual, gate_scale):
     bias, gate = out_bias, gate_scale
+    owners, starts, bars, longest = tile_lists(tile_mask)
 
     def by_lists(_):
-        owners, starts, bars = tile_lists(tile_mask)
         return whole(owners, starts, bars, queries, key_states, value_states, out_weight, bias, gate, residual)
 
     def in_parts(_):
@@ -1022,8 +1057,7 @@
         o = attend(tile_mask, q, kv)
         return project(o, panel.reshape(RING * ROWS, 2 * ROWS), bias[None, :], gate[None, :], residual)
 
-    longest = jnp.max(jnp.sum((tile_mask > 0).astype(jnp.int32), axis=1))
-    return lax.cond(longest <= LIMIT, by_lists, in_parts, 0)
+    return lax.cond(longest[0] <= LIMIT, by_lists, in_parts, 0)
 
 
 def solution(mesh):

time: 118 us -> 113 us (0.958)
  other arithmetic: 3.5 us -> 0 us
    pallas_call x1, Pallas kernels: 112 us -> 109 us  [whole(): pl.pallas_call(whole_kernel, out_shape=jax.ShapeDtypeStruct((ROWS, ROWS),...]
    pallas_call x0 -> x1, Pallas kernels: none -> 1.73 us  [tile_lists(): pl.pallas_call(list_kernel, out_shape=[jax.ShapeDtypeStruct((LIMIT, 128),...]
    reduce_sum x4 -> x0, other arithmetic: 1.57 us -> none  [the longest x1 0.88 us: local(): longest = jnp.max(jnp.sum((tile_mask > 0).astype(jnp.int32), axis=1))]
    select_n x2 -> x0, other arithmetic: 1.28 us -> none  [the longest x1 0.66 us: tile_lists(): jnp.where(at[None, :LIMIT] < jnp.sum(allowed, axis=1)[:, None], 0.0, MASKED)]
where the time goes in v5:
time: 113 us
  Pallas kernels  111 us (98%)
    pallas_call x1, Pallas kernels, whole(): pl.pallas_call(whole_kernel, out_shape=jax.ShapeDtypeStruct((ROWS, ROWS),...  109 us

profile of v5, /device:TPU:0, one launch (start us, length us, event | category | flops | bytes accessed | tf_op | source)
XLA Modules:
  0.0 113.2 jit_solution(12550613368174154172)
XLA Ops:
  0.0 1.7 %tile_lists.1 = (s32[40,128]{1,0:T(8,128)S(1)}, s32[40,128]{1,0:T(8,128)S(1)}, f32[40,128]{1,0:T(8,128)S(1)}, s32[1]{0:T(128)}) custom-call(s32[80,80]{1,0:T(8,128)} %mask_ref.1), custom_call_target="tpu_custom_call" | custom-call | tf_op jit(solution)/shard_map/tile_lists/pallas_call | solution.py:1034
  2.4 109.9 %conditional.1 = (bf16[640,640]{1,0:T(8,128)(2,1)S(1)}) conditional(s32[]{:T(128)} %bitcast.4, (bf16[640,640]{1,0:T(8,128)(2,1)}, bf16[640,640]{1,0:T(8,128)(2,1)}, bf16[640,640]{1,0:T(8,128)(2,1)}, bf16[640,5120]{1,0:T(8,128)(2,1)}, s32[80,80]{1,0:T(8,128)}, /*index=5*/f32[640]{0:T(1024)}, f32[640]{0:T(1024)}, bf16[640,640]{1,0:T(8,128)(2,1)}) %tuple.11, ...), branch_computations={%region_0.0_spmd, %region_1.0_spmd} | conditional | bytes 3410040 | solution.py:1060
  2.6 109.4 %whole.1 = bf16[640,640]{1,0:T(8,128)(2,1)S(1)} custom-call(s32[40,128]{1,0:T(8,128)S(1)} %get-tuple-element.55.owners_ref, s32[40,128]{1,0:T(8,128)S(1)} %get-tuple-element.56.starts_ref, f32[40,128]{1,0:T(8,128)S(1)} %get-tuple-element.57.bars_ref, bf16[5,128,640]{2,1,0:T(8,128)(2,1)} %bitcast.6, bf16[5,128,640]{2,1,0:T(8,128)(2,1)} %bitcast.7, ...), custom_call_target="tpu_custom_call" | custom-call | tf_op jit(solution)/shard_map/cond/branch_1_fun/whole/pallas_call | solution.py:966
  112.3 0.9 copy.14

commit v6 on v5

--- a/solution.py
+++ b/solution.py
@@ -781,9 +781,9 @@
 
     positions = [own_a, own_a + 1, pair_a, pair_a + 1, 4]
 
-    row_groups = {0: [(0, 640)], 1: [(0, 384), (384, 256)], 2: [(0, 640)], 3: [(0, 384), (384, 256)]}
+    row_groups = {0: [(0, 640)], 1: [(0, 256), (256, 256), (512, 128)], 2: [(0, 640)], 3: [(0, 256), (256, 256), (512, 128)]}
     row_groups[4] = [(TILE * i, TILE) for i in range(ROW_TILES)]
-    first_sem = {0: 0, 1: 1, 2: 3, 3: 4, 4: 6}
+    first_sem = {0: 0, 1: 1, 2: 4, 3: 5, 4: 8}
 
     def y_block(n, y_, start, count):
         return att.at[y_, positions[n], pl.ds(start, count)]
@@ -883,13 +883,22 @@
         to_sibling("h", kvh, other, right, v_part)
         y_pass(2)
 
-    def after_b2():
-        give_back(1, 0)
-        y_send(1, 0)
-
-    attention(kvb, plan_of(1), {1: after_b1, 2: after_b2, 3: after_b3})
-    give_back(1, 1)
-    y_send(1, 1)
+    def hand_out_b(g):
+        give_back(1, g)
+        y_send(1, g)
+
+    def after_b1_too():
+        hand_out_b(0)
+        after_b1()
+
+    def after_b3_too():
+        hand_out_b(1)
+        after_b3()
+        given_back(1, 0)
+        y_pass(1, 0)
+
+    attention(kvb, plan_of(1), {1: after_b1_too, 3: after_b3_too}, 2 * GROUP)
+    hand_out_b(2)
     ring_far(H0, "h", kvh, zl)
     send(block(kvh, zl, opposite, k_part), block(kvh, zl, opposite, k_part), z_sem.at[6], to_pair)
     arrived(v_block(opposite, v_first), far_sem.at[0, V1], to_left)
@@ -898,19 +907,20 @@
     for n, x_ in ((4, left), (5, right)):
         arrived(block(kvh, other, x_, k_part), z_sem.at[n], to_pair)
         to_sibling("h", kvh, other, x_, k_part)
-    given_back(1, 0)
-    y_pass(1, 0)
+    given_back(1, 1)
+    y_pass(1, 1)
     y_far(0)
     y_far(2)
     for d in range(RING):
         arrived(panel.at[lax.rem(y + d, RING), other_half], w_sib_sem.at[d], to_sib)
     contract((0, 2), True, ((theirs, theirs_columns), (mine, ours_columns)))
-    given_back(1, 1)
+    given_back(1, 2)
     arrived(block(kvh, other, opposite, k_part), z_sem.at[6], to_pair)
     to_sibling("h", kvh, other, opposite, k_part)
-    y_pass(1, 1)
+    y_pass(1, 2)
     y_pass(3, 0)
     from_sibling("h")
+    y_pass(3, 1)
 
     units = [
         (i, (q_own, 2, i), (att.at[y, 4], tile_rows(i))) for i in range(ROW_TILES)
@@ -925,12 +935,12 @@
     def after_h(i):
         y_send(4, i)
         if i == 0:
-            y_pass(3, 1)
+            y_pass(3, 2)
         else:
             y_pass(4, i - 1)
         if i == 2:
             for n in (1, 3):
-                for g in range(2):
+                for g in range(3):
                     y_far(n, g)
         if i >= 2:
             sum_out(i - 2)
@@ -988,8 +998,8 @@
         + [pltpu.VMEM((LIMIT, TILE, TILE), f32)] * 4
         + [pltpu.VMEM((HEAD_DIM, TILE), f32)] * 2
         + [
-            dma((12,)), dma((8,)), dma((128,)), dma((7,)), dma((2, 6)), dma((2, 6)), dma((28,)), dma((3,)), dma((4,)),
-            dma((3,)), dma((2, 11)), dma((2, 11)), dma((5,)),
+            dma((12,)), dma((8,)), dma((160,)), dma((7,)), dma((2, 6)), dma((2, 6)), dma((28,)), dma((3,)), dma((4,)),
+            dma((4,)), dma((2, 13)), dma((2, 13)), dma((5,)),
         ],
         compiler_params=pltpu.CompilerParams(collective_id=2, has_side_effects=True, vmem_limit_bytes=62 << 20),
         name="whole",

time: 113 us -> 113 us (level)
  no operation moved by 1% of the time
where the time goes in v6:
time: 113 us
  Pallas kernels  110 us (97%)
    pallas_call x1, Pallas kernels, whole(): pl.pallas_call(whole_kernel, out_shape=jax.ShapeDtypeStruct((ROWS, ROWS),...  109 us

profile of v6, /device:TPU:0, one launch (start us, length us, event | category | flops | bytes accessed | tf_op | source)
XLA Modules:
  0.0 112.5 jit_solution(13538465515805567825)
XLA Ops:
  0.0 1.7 %tile_lists.1 = (s32[40,128]{1,0:T(8,128)S(1)}, s32[40,128]{1,0:T(8,128)S(1)}, f32[40,128]{1,0:T(8,128)S(1)}, s32[1]{0:T(128)}) custom-call(s32[80,80]{1,0:T(8,128)} %mask_ref.1), custom_call_target="tpu_custom_call" | custom-call | tf_op jit(solution)/shard_map/tile_lists/pallas_call | solution.py:1044
  2.4 109.3 %conditional.1 = (bf16[640,640]{1,0:T(8,128)(2,1)S(1)}) conditional(s32[]{:T(128)} %bitcast.4, (bf16[640,640]{1,0:T(8,128)(2,1)}, bf16[640,640]{1,0:T(8,128)(2,1)}, bf16[640,640]{1,0:T(8,128)(2,1)}, bf16[640,5120]{1,0:T(8,128)(2,1)}, s32[80,80]{1,0:T(8,128)}, /*index=5*/f32[640]{0:T(1024)}, f32[640]{0:T(1024)}, bf16[640,640]{1,0:T(8,128)(2,1)}) %tuple.11, ...), branch_computations={%region_0.0_spmd, %region_1.0_spmd} | conditional | bytes 3410040 | solution.py:1070
  2.6 108.7 %whole.1 = bf16[640,640]{1,0:T(8,128)(2,1)S(1)} custom-call(s32[40,128]{1,0:T(8,128)S(1)} %get-tuple-element.55.owners_ref, s32[40,128]{1,0:T(8,128)S(1)} %get-tuple-element.56.starts_ref, f32[40,128]{1,0:T(8,128)S(1)} %get-tuple-element.57.bars_ref, bf16[5,128,640]{2,1,0:T(8,128)(2,1)} %bitcast.6, bf16[5,128,640]{2,1,0:T(8,128)(2,1)} %bitcast.7, ...), custom_call_target="tpu_custom_call" | custom-call | tf_op jit(solution)/shard_map/cond/branch_1_fun/whole/pallas_call | solution.py:976
  111.7 0.9 copy.14
